TPU v7x, 32 devices: a whole 2x2x4 slice. The times are simulated.
32 devices in a mesh: seq: 16 (over z, y, x), tp: 2 (over core).
Axes of the slice: x: 2, y: 2, z: 4, core: 2. Of those that a mesh axis runs over, the one named last changes fastest.
Arguments:
- tokens: bfloat16 [4096, 1536], P('seq'), may hold values from -6 to 6
- cotangent: bfloat16 [4096, 1536], P('seq'), may hold values from -6 to 6
- step_embed: bfloat16 [4, 1024], replicated, may hold values from -6 to 6
- item_band: int32 [4], replicated, may hold values from 0 to 3, as said below
- item_length: int32 [4], replicated, may hold values from 512 to 1024, as said below
- item_width: int32 [4], replicated, may hold values from 16 to 64
- text_states: bfloat16 [1024, 4096], P('seq'), may hold values from -6 to 6
- ada_weight: bfloat16 [1024, 6144], P(None, 'tp'), may hold values from -0.1875 to 0.1875
- ada_bias: float32 [6144], P('tp'), may hold values from -1.5 to 1.5
- attn_gain: float32 [1536], replicated, may hold values from 0.5 to 1.5
- ffn_gain: float32 [1536], replicated, may hold values from 0.5 to 1.5
- query_weight: bfloat16 [1536, 1536], P(None, 'tp'), may hold values from -0.15625 to 0.15625
- key_weight: bfloat16 [1536, 1536], P(None, 'tp'), may hold values from -0.15625 to 0.15625
- value_weight: bfloat16 [1536, 1536], P(None, 'tp'), may hold values from -0.15625 to 0.15625
- query_gain: float32 [1536], P('tp'), may hold values from 1 to 2
- key_gain: float32 [1536], P('tp'), may hold values from 1 to 2
- cross_gate: float32 [24], P('tp'), may hold values from 0.3 to 1.2
- text_key_weight: bfloat16 [4096, 1536], P(None, 'tp'), may hold values from -0.09375 to 0.09375
- text_value_weight: bfloat16 [4096, 1536], P(None, 'tp'), may hold values from -0.09375 to 0.09375
- text_key_gain: float32 [1536], P('tp'), may hold values from 1 to 2
- out_weight: bfloat16 [1536, 1536], P('tp'), may hold values from -3.5 to 3.5
- gate_weight: bfloat16 [1536, 4096], P(None, 'tp'), may hold values from -0.15625 to 0.15625
- up_weight: bfloat16 [1536, 4096], P(None, 'tp'), may hold values from -0.15625 to 0.15625
- down_weight: bfloat16 [4096, 1536], P('tp'), may hold values from -0.09375 to 0.09375
Outputs:
- block_out: bfloat16 [4096, 1536], P('seq')
- tokens_grad: bfloat16 [4096, 1536], P('seq')
- text_grad: float32 [1024, 4096], P('seq', 'tp')
- ada_weight_grad: float32 [1024, 6144], P('seq', 'tp')
- ada_bias_grad: float32 [6144], P('tp')
- attn_gain_grad: float32 [1536], replicated
- ffn_gain_grad: float32 [1536], replicated
- query_weight_grad: float32 [1536, 1536], P('seq', 'tp')
- key_weight_grad: float32 [1536, 1536], P('seq', 'tp')
- value_weight_grad: float32 [1536, 1536], P('seq', 'tp')
- query_gain_grad: float32 [1536], P('tp')
- key_gain_grad: float32 [1536], P('tp')
- cross_gate_grad: float32 [24], P('tp')
- text_key_weight_grad: float32 [4096, 1536], P('seq', 'tp')
- text_value_weight_grad: float32 [4096, 1536], P('seq', 'tp')
- text_key_gain_grad: float32 [1536], P('tp')
- out_weight_grad: float32 [1536, 1536], P('tp', 'seq')
- gate_weight_grad: float32 [1536, 4096], P('seq', 'tp')
- up_weight_grad: float32 [1536, 4096], P('seq', 'tp')
- down_weight_grad: float32 [4096, 1536], P('tp', 'seq')
Inputs may be any that keep to these rules, and one draw needn't show every extreme that they name: `item_band`: every band is used by some item. Item i's real tokens are its first item_length[i] positions; one item fills all 1024 positions and another has exactly 512.
All inputs are finite; a program needn't handle non-finite values.
Results may differ from a plain program's by a relative error of at most 0.024.
Values may be sent and summed in bfloat16 or wider, within the bound.
No kernel may reach another device: no remote copies, remote signals or barrier semaphores. Data moves between devices by JAX's collectives and lax.ppermute only.
A program may use at most 256 MiB of HBM per device.

v0:
```python
import jax
import jax.numpy as jnp
from jax import lax
from jax.experimental import pallas as pl
from jax.experimental.pallas import tpu as pltpu
from jax.sharding import Mesh
from jax.sharding import PartitionSpec as P

HDIM = 64
NTXT = 256
BANDS = 4
ITEMS = 4
SLOT = 64


EPSILON = 1e-06
ROPE_BASE = 10000.0
HIGHEST = lax.Precision.HIGHEST
NEG_FILL = -1e30


def rms_inverse(values):
    return lax.rsqrt(jnp.mean(values * values, axis=-1, keepdims=True) + EPSILON)


def rope_angles(row_pos, col_pos, head_dim):
    quarter = head_dim // 4
    frequency = ROPE_BASE ** (-jnp.arange(quarter, dtype=jnp.float32) / quarter)
    angles = jnp.stack([row_pos[..., None] * frequency, col_pos[..., None] * frequency], axis=-2)
    return (jnp.cos(angles), jnp.sin(angles))


def rotate(vectors, cosines, sines):
    shape_all = vectors.shape
    paired = vectors.reshape(shape_all[:-1] + (2, 2, shape_all[-1] // 4))
    former = paired[..., 0, :]
    latter = paired[..., 1, :]
    turned = jnp.stack(
        [former * cosines - latter * sines, former * sines + latter * cosines], axis=-2
    )
    return turned.reshape(shape_all)


def head_norm(raw_vals, gain_vec):
    inverse = rms_inverse(raw_vals)
    unit_vec = raw_vals * inverse
    return (unit_vec * gain_vec, unit_vec, inverse)


def head_norm_back(incoming, unit_vec, inverse, gain_vec):
    grad_unit = incoming * gain_vec
    gain_part = jnp.sum(incoming * unit_vec, axis=tuple(range(incoming.ndim - 2)))
    grad_raw = inverse * (
        grad_unit - unit_vec * jnp.mean(grad_unit * unit_vec, axis=-1, keepdims=True)
    )
    return (grad_raw, gain_part)


def token_norm_back(incoming, normed, inverse, gain_vec, scale_mod):
    lifted = 1.0 + scale_mod
    gain_part = jnp.sum(incoming * normed * lifted, axis=(0, 1))
    scale_part = jnp.sum(incoming * normed * gain_vec, axis=1)
    grad_normed = incoming * gain_vec * lifted
    grad_in = inverse * (
        grad_normed - normed * jnp.mean(grad_normed * normed, axis=-1, keepdims=True)
    )
    return (grad_in, gain_part, scale_part)


def attend(query_h, key_h, value_h, key_valid):
    scaling = query_h.shape[-1] ** (-0.5)
    scores = (
        jnp.einsum("isd,ikd->isk", query_h, key_h, preferred_element_type=jnp.float32) * scaling
    )
    if key_valid is not None:
        scores = jnp.where(key_valid[:, None, :], scores, NEG_FILL)
    row_max = jnp.max(scores, axis=-1, keepdims=True)
    exp_scores = jnp.exp(scores - row_max)
    row_total = jnp.sum(exp_scores, axis=-1, keepdims=True)
    probability = (exp_scores / row_total).astype(jnp.bfloat16)
    output = jnp.einsum("isk,ikd->isd", probability, value_h, preferred_element_type=jnp.float32)
    return (output, (row_max + jnp.log(row_total))[..., 0])


def attend_back(query_h, key_h, value_h, key_valid, lse_h, dout_h):
    scaling = query_h.shape[-1] ** (-0.5)
    scores = (
        jnp.einsum("isd,ikd->isk", query_h, key_h, preferred_element_type=jnp.float32) * scaling
    )
    if key_valid is not None:
        scores = jnp.where(key_valid[:, None, :], scores, NEG_FILL)
    probability = jnp.exp(scores - lse_h[..., None])
    d_prob = jnp.einsum("isd,ikd->isk", dout_h, value_h, preferred_element_type=jnp.float32)
    delta_row = jnp.sum(d_prob * probability, axis=-1)
    d_score = (probability * (d_prob - delta_row[..., None])).astype(jnp.bfloat16)
    d_query = (
        jnp.einsum("isk,ikd->isd", d_score, key_h, preferred_element_type=jnp.float32) * scaling
    )
    d_key = (
        jnp.einsum("isk,isd->ikd", d_score, query_h, preferred_element_type=jnp.float32) * scaling
    )
    d_value = jnp.einsum(
        "isk,isd->ikd", probability.astype(jnp.bfloat16), dout_h, preferred_element_type=jnp.float32
    )
    return (d_query, delta_row, d_key, d_value)


def head_total(partial_value):
    return lax.psum(partial_value.astype(jnp.bfloat16), "tp").astype(jnp.float32)


def feature_total(partial_value):
    return lax.psum(partial_value.astype(jnp.bfloat16), "tp").astype(jnp.float32)


def shards(
    tokens,
    cotangent,
    step_embed,
    item_band,
    item_length,
    item_width,
    text_states,
    ada_weight,
    ada_bias,
    attn_gain,
    ffn_gain,
    query_weight,
    key_weight,
    value_weight,
    query_gain,
    key_gain,
    cross_gate,
    text_key_weight,
    text_value_weight,
    text_key_gain,
    out_weight,
    gate_weight,
    up_weight,
    down_weight,
):
    seq_count = lax.axis_size("seq")
    seq_index = lax.axis_index("seq")
    tp_index = lax.axis_index("tp")
    tok_dev, model_width = tokens.shape
    local_width = query_weight.shape[1]
    local_heads = local_width // HDIM
    capacity = SLOT * seq_count
    text_rows = text_states.shape[0]
    mod_cols = ada_weight.shape[1]
    head_shape = (ITEMS, SLOT, local_heads, HDIM)
    silu_embed = jax.nn.silu(step_embed.astype(jnp.float32))
    local_mod = jnp.dot(silu_embed, ada_weight.astype(jnp.float32), precision=HIGHEST) + ada_bias
    band_mod = lax.all_gather(local_mod, "tp", axis=1, tiled=True)
    band_onehot = (item_band[:, None] == jnp.arange(BANDS, dtype=jnp.int32)[None, :]).astype(
        jnp.float32
    )
    item_mod = jnp.dot(band_onehot, band_mod, precision=HIGHEST)
    scale_attn = item_mod[:, None, 0:model_width]
    gate_attn = jnp.tanh(item_mod[:, None, model_width : 2 * model_width])
    scale_ffn = item_mod[:, None, 2 * model_width : 3 * model_width]
    gate_ffn = jnp.tanh(item_mod[:, None, 3 * model_width :])
    slot_pos = seq_index * SLOT + jnp.arange(SLOT, dtype=jnp.int32)
    row_pos = (slot_pos[None, :] // item_width[:, None]).astype(jnp.float32)
    col_pos = (slot_pos[None, :] % item_width[:, None]).astype(jnp.float32)
    cosines, sines = rope_angles(row_pos, col_pos, HDIM)
    cosines = cosines[:, :, None]
    sines = sines[:, :, None]
    key_valid = jnp.arange(capacity, dtype=jnp.int32)[None, :] < item_length[:, None]

    def by_heads(array_in, row_count):
        return jnp.moveaxis(array_in.reshape(ITEMS, row_count, local_heads, HDIM), 2, 0)

    text_key_raw = jnp.dot(
        text_states, text_key_weight, preferred_element_type=jnp.float32
    ).reshape(text_rows, local_heads, HDIM)
    text_gain_vec = text_key_gain.reshape(local_heads, HDIM)
    text_key_normed, text_unit, text_inverse = head_norm(text_key_raw, text_gain_vec)
    text_key_low = text_key_normed.reshape(text_rows, local_width).astype(jnp.bfloat16)
    text_value_low = jnp.dot(
        text_states, text_value_weight, preferred_element_type=jnp.float32
    ).astype(jnp.bfloat16)
    text_key_all, text_value_all = (
        lax.all_gather(text_key_low, "seq", axis=0, tiled=True),
        lax.all_gather(text_value_low, "seq", axis=0, tiled=True),
    )
    residual = tokens.astype(jnp.float32).reshape(ITEMS, SLOT, model_width)
    inverse_one = rms_inverse(residual)
    normed_one = residual * inverse_one
    attn_in = (
        (normed_one * attn_gain * (1.0 + scale_attn))
        .astype(jnp.bfloat16)
        .reshape(tok_dev, model_width)
    )
    query_raw = jnp.dot(attn_in, query_weight, preferred_element_type=jnp.float32).reshape(
        head_shape
    )
    key_raw = jnp.dot(attn_in, key_weight, preferred_element_type=jnp.float32).reshape(head_shape)
    value_low = (
        jnp.dot(attn_in, value_weight, preferred_element_type=jnp.float32)
        .astype(jnp.bfloat16)
        .reshape(ITEMS, SLOT, local_width)
    )
    query_gain_vec = query_gain.reshape(local_heads, HDIM)
    key_gain_vec = key_gain.reshape(local_heads, HDIM)
    query_normed, query_unit, query_inverse = head_norm(query_raw, query_gain_vec)
    key_normed, key_unit, key_inverse = head_norm(key_raw, key_gain_vec)
    query_low = rotate(query_normed, cosines, sines).astype(jnp.bfloat16)
    key_low = (
        rotate(key_normed, cosines, sines).astype(jnp.bfloat16).reshape(ITEMS, SLOT, local_width)
    )
    key_all, value_all = (
        lax.all_gather(key_low, "seq", axis=1, tiled=True),
        lax.all_gather(value_low, "seq", axis=1, tiled=True),
    )
    query_heads = jnp.moveaxis(query_low, 2, 0)
    key_heads = by_heads(key_all, capacity)
    value_heads = by_heads(value_all, capacity)
    text_key_heads = by_heads(text_key_all, NTXT)
    text_value_heads = by_heads(text_value_all, NTXT)

    def forward_head(operands):
        query_h, key_h, value_h, tkey_h, tvalue_h = operands
        self_part, self_stat = attend(query_h, key_h, value_h, key_valid)
        cross_part, cross_stat = attend(query_h, tkey_h, tvalue_h, None)
        return (self_part, self_stat, cross_part, cross_stat)

    self_out, self_lse, cross_out, cross_lse = lax.map(
        forward_head, (query_heads, key_heads, value_heads, text_key_heads, text_value_heads)
    )
    cross_tanh = jnp.tanh(cross_gate)
    combined = self_out + cross_tanh[:, None, None, None] * cross_out
    combined_low = jnp.moveaxis(combined, 0, 2).reshape(tok_dev, local_width).astype(jnp.bfloat16)
    attn_branch = head_total(
        jnp.dot(combined_low, out_weight, preferred_element_type=jnp.float32)
    ).reshape(ITEMS, SLOT, model_width)
    middle = residual + gate_attn * attn_branch
    inverse_two = rms_inverse(middle)
    normed_two = middle * inverse_two
    ffn_in = (
        (normed_two * ffn_gain * (1.0 + scale_ffn))
        .astype(jnp.bfloat16)
        .reshape(tok_dev, model_width)
    )
    gate_pre = jnp.dot(ffn_in, gate_weight, preferred_element_type=jnp.float32)
    up_pre = jnp.dot(ffn_in, up_weight, preferred_element_type=jnp.float32)
    gate_sig = jax.nn.sigmoid(gate_pre)
    hidden = (gate_pre * gate_sig * up_pre).astype(jnp.bfloat16)
    ffn_branch = head_total(
        jnp.dot(hidden, down_weight, preferred_element_type=jnp.float32)
    ).reshape(ITEMS, SLOT, model_width)
    layer_sum = middle + gate_ffn * ffn_branch
    block_out = layer_sum.reshape(tok_dev, model_width).astype(jnp.bfloat16)
    incoming = cotangent.astype(jnp.float32).reshape(ITEMS, SLOT, model_width)
    gate_ffn_tok = incoming * ffn_branch
    d_ffn = (gate_ffn * incoming).reshape(tok_dev, model_width).astype(jnp.bfloat16)
    down_grad = jnp.dot(hidden.T, d_ffn, preferred_element_type=jnp.float32)
    d_hidden = jnp.dot(d_ffn, down_weight.T, preferred_element_type=jnp.float32)
    d_gate_pre = (d_hidden * up_pre * gate_sig * (1.0 + gate_pre * (1.0 - gate_sig))).astype(
        jnp.bfloat16
    )
    d_up_pre = (d_hidden * gate_pre * gate_sig).astype(jnp.bfloat16)
    gate_grad = jnp.dot(ffn_in.T, d_gate_pre, preferred_element_type=jnp.float32)
    up_grad = jnp.dot(ffn_in.T, d_up_pre, preferred_element_type=jnp.float32)
    d_ffn_in = feature_total(
        jnp.dot(d_gate_pre, gate_weight.T, preferred_element_type=jnp.float32)
        + jnp.dot(d_up_pre, up_weight.T, preferred_element_type=jnp.float32)
    )
    d_middle_norm, ffn_gain_part, scale_ffn_part = token_norm_back(
        d_ffn_in.reshape(ITEMS, SLOT, model_width), normed_two, inverse_two, ffn_gain, scale_ffn
    )
    d_middle = incoming + d_middle_norm
    gate_attn_tok = d_middle * attn_branch
    d_attn = (gate_attn * d_middle).reshape(tok_dev, model_width).astype(jnp.bfloat16)
    out_grad = jnp.dot(combined_low.T, d_attn, preferred_element_type=jnp.float32)
    d_combined = jnp.moveaxis(
        jnp.dot(d_attn, out_weight.T, preferred_element_type=jnp.float32).reshape(head_shape), 2, 0
    )
    cross_gate_part = jnp.sum(d_combined * cross_out, axis=(1, 2, 3)) * (
        1.0 - cross_tanh * cross_tanh
    )
    d_self = d_combined.astype(jnp.bfloat16)
    d_cross = (d_combined * cross_tanh[:, None, None, None]).astype(jnp.bfloat16)

    def cross_head(operands):
        query_h, tkey_h, tvalue_h, lse_h, dout_h = operands
        d_query, unused_delta, d_key, d_value = attend_back(
            query_h, tkey_h, tvalue_h, None, lse_h, dout_h
        )
        return (d_query, d_key, d_value)

    d_query_cross, d_text_key_heads, d_text_value_heads = lax.map(
        cross_head, (query_heads, text_key_heads, text_value_heads, cross_lse, d_cross)
    )

    def full_head(operands):
        query_h, key_h, value_h, lse_h, dout_h = operands
        d_query, unused_delta, d_key, d_value = attend_back(
            query_h, key_h, value_h, key_valid, lse_h, dout_h
        )
        return (d_query, d_key, d_value)

    d_query_self, d_key_heads, d_value_heads = lax.map(
        full_head, (query_heads, key_heads, value_heads, self_lse, d_self)
    )
    d_key_own, d_value_own = (
        lax.psum_scatter(
            jnp.moveaxis(d_key_heads, 0, 2)
            .reshape(ITEMS, capacity, local_width)
            .astype(jnp.bfloat16),
            "seq",
            scatter_dimension=1,
            tiled=True,
        ).astype(jnp.float32),
        lax.psum_scatter(
            jnp.moveaxis(d_value_heads, 0, 2)
            .reshape(ITEMS, capacity, local_width)
            .astype(jnp.bfloat16),
            "seq",
            scatter_dimension=1,
            tiled=True,
        ).astype(jnp.float32),
    )
    d_key_rot = d_key_own.reshape(head_shape)
    d_query_rot = jnp.moveaxis(d_query_self + d_query_cross, 0, 2)
    d_query_raw, query_gain_part = head_norm_back(
        rotate(d_query_rot, cosines, -sines), query_unit, query_inverse, query_gain_vec
    )
    d_key_raw, key_gain_part = head_norm_back(
        rotate(d_key_rot, cosines, -sines), key_unit, key_inverse, key_gain_vec
    )
    d_query_low = d_query_raw.reshape(tok_dev, local_width).astype(jnp.bfloat16)
    d_key_low = d_key_raw.reshape(tok_dev, local_width).astype(jnp.bfloat16)
    d_value_low = d_value_own.reshape(tok_dev, local_width).astype(jnp.bfloat16)
    query_grad = jnp.dot(attn_in.T, d_query_low, preferred_element_type=jnp.float32)
    key_grad = jnp.dot(attn_in.T, d_key_low, preferred_element_type=jnp.float32)
    value_grad = jnp.dot(attn_in.T, d_value_low, preferred_element_type=jnp.float32)
    d_attn_in = feature_total(
        jnp.dot(d_query_low, query_weight.T, preferred_element_type=jnp.float32)
        + jnp.dot(d_key_low, key_weight.T, preferred_element_type=jnp.float32)
        + jnp.dot(d_value_low, value_weight.T, preferred_element_type=jnp.float32)
    )
    d_input_norm, attn_gain_part, scale_attn_part = token_norm_back(
        d_attn_in.reshape(ITEMS, SLOT, model_width), normed_one, inverse_one, attn_gain, scale_attn
    )
    tokens_grad = (d_middle + d_input_norm).reshape(tok_dev, model_width).astype(jnp.bfloat16)
    d_text_key_own, d_text_value_own = (
        lax.psum_scatter(
            jnp.moveaxis(d_text_key_heads, 0, 2)
            .reshape(ITEMS * NTXT, local_width)
            .astype(jnp.bfloat16),
            "seq",
            scatter_dimension=0,
            tiled=True,
        ).astype(jnp.float32),
        lax.psum_scatter(
            jnp.moveaxis(d_text_value_heads, 0, 2)
            .reshape(ITEMS * NTXT, local_width)
            .astype(jnp.bfloat16),
            "seq",
            scatter_dimension=0,
            tiled=True,
        ).astype(jnp.float32),
    )
    d_text_key_raw, text_gain_part = head_norm_back(
        d_text_key_own.reshape(text_rows, local_heads, HDIM), text_unit, text_inverse, text_gain_vec
    )
    d_text_key_low = d_text_key_raw.reshape(text_rows, local_width).astype(jnp.bfloat16)
    d_text_value_low = d_text_value_own.astype(jnp.bfloat16)
    text_key_grad = jnp.dot(text_states.T, d_text_key_low, preferred_element_type=jnp.float32)
    text_value_grad = jnp.dot(text_states.T, d_text_value_low, preferred_element_type=jnp.float32)
    text_grad = lax.psum_scatter(
        (
            jnp.dot(d_text_key_low, text_key_weight.T, preferred_element_type=jnp.float32)
            + jnp.dot(d_text_value_low, text_value_weight.T, preferred_element_type=jnp.float32)
        ).astype(jnp.bfloat16),
        "tp",
        scatter_dimension=1,
        tiled=True,
    ).astype(jnp.float32)
    gate_attn_item = jnp.sum(gate_attn_tok, axis=1) * (1.0 - gate_attn[:, 0] * gate_attn[:, 0])
    gate_ffn_item = jnp.sum(gate_ffn_tok, axis=1) * (1.0 - gate_ffn[:, 0] * gate_ffn[:, 0])
    item_grad = jnp.concatenate(
        [scale_attn_part, gate_attn_item, scale_ffn_part, gate_ffn_item], axis=1
    )
    band_grad = jnp.dot(band_onehot.T, item_grad, precision=HIGHEST)
    local_band_grad = lax.dynamic_slice_in_dim(band_grad, tp_index * mod_cols, mod_cols, 1)
    ada_grad = jnp.dot(silu_embed.T, local_band_grad, precision=HIGHEST)
    ada_bias_part = jnp.sum(local_band_grad, axis=0)
    summed = (
        lax.psum_scatter(
            query_grad.astype(jnp.bfloat16), "seq", scatter_dimension=0, tiled=True
        ).astype(jnp.float32),
        lax.psum_scatter(
            key_grad.astype(jnp.bfloat16), "seq", scatter_dimension=0, tiled=True
        ).astype(jnp.float32),
        lax.psum_scatter(
            value_grad.astype(jnp.bfloat16), "seq", scatter_dimension=0, tiled=True
        ).astype(jnp.float32),
        lax.psum_scatter(
            gate_grad.astype(jnp.bfloat16), "seq", scatter_dimension=0, tiled=True
        ).astype(jnp.float32),
        lax.psum_scatter(
            up_grad.astype(jnp.bfloat16), "seq", scatter_dimension=0, tiled=True
        ).astype(jnp.float32),
        lax.psum_scatter(
            text_key_grad.astype(jnp.bfloat16), "seq", scatter_dimension=0, tiled=True
        ).astype(jnp.float32),
        lax.psum_scatter(
            text_value_grad.astype(jnp.bfloat16), "seq", scatter_dimension=0, tiled=True
        ).astype(jnp.float32),
        lax.psum_scatter(
            ada_grad.astype(jnp.bfloat16), "seq", scatter_dimension=0, tiled=True
        ).astype(jnp.float32),
        lax.psum_scatter(
            out_grad.astype(jnp.bfloat16), "seq", scatter_dimension=1, tiled=True
        ).astype(jnp.float32),
        lax.psum_scatter(
            down_grad.astype(jnp.bfloat16), "seq", scatter_dimension=1, tiled=True
        ).astype(jnp.float32),
    )
    smalls = lax.psum(
        (
            attn_gain_part,
            ffn_gain_part,
            query_gain_part.reshape(local_width),
            key_gain_part.reshape(local_width),
            text_gain_part.reshape(local_width),
            cross_gate_part,
            ada_bias_part,
        ),
        "seq",
    )
    return (
        block_out,
        tokens_grad,
        text_grad,
        summed[7],
        smalls[6],
        smalls[0],
        smalls[1],
        summed[0],
        summed[1],
        summed[2],
        smalls[2],
        smalls[3],
        smalls[5],
        summed[5],
        summed[6],
        smalls[4],
        summed[8],
        summed[3],
        summed[4],
        summed[9],
    )


MESH_AXES = ("z", "y", "x", "c")
PLANE_AXES = ("y", "x")
PLANE = 4
STRIPS = 4
CORES = 2


def device_pairs(target):
    pairs = []
    for strip in range(STRIPS):
        for place in range(PLANE):
            for core in range(CORES):
                aim = target(strip, place, core)
                pairs.append(
                    (
                        (strip * PLANE + place) * CORES + core,
                        (aim[0] * PLANE + aim[1]) * CORES + aim[2],
                    )
                )
    return pairs


FLIP_CORE = device_pairs(lambda strip, place, core: (strip, place, 1 - core))
FLIP_FIRST = device_pairs(lambda strip, place, core: (strip, place ^ (1 + core), core))
FLIP_SECOND = device_pairs(lambda strip, place, core: (strip, place ^ (2 - core), core))
FLIP_PLACE = {
    mask: device_pairs(lambda strip, place, core, mask=mask: (strip, place ^ mask, core))
    for mask in (1, 2, 3)
}
FLIP_STRIP = {
    mask: device_pairs(lambda strip, place, core, mask=mask: (strip ^ mask, place, core))
    for mask in (1, 2, 3)
}


def move(value, pairs):
    return lax.ppermute(value, MESH_AXES, pairs)


def gather_by(value, table):
    return [value] + [move(value, table[mask]) for mask in (1, 2, 3)]


def after(value, *earlier):
    return lax.optimization_barrier((value, earlier))[0]


def plane_gather(own, beside=()):
    own = jnp.concatenate([own, move(own, FLIP_FIRST)])
    own = jnp.concatenate([own, after(move(own, FLIP_SECOND), beside)])
    return own, move(own, FLIP_CORE)


SCATTER_STEPS = (FLIP_CORE, FLIP_SECOND, FLIP_FIRST)


def core_half(whole):
    half = whole.shape[0] // 2
    arrived = move(whole[half:], FLIP_CORE)
    return whole[:half].astype(jnp.float32) + arrived.astype(jnp.float32)


def plane_scatter(whole, *besides):
    for step, pairs in enumerate(SCATTER_STEPS[-(whole.shape[0] // 256).bit_length() :]):
        half = whole.shape[0] // 2
        arrived = move(whole[half:].astype(jnp.bfloat16), pairs)
        if step < len(besides):
            arrived = after(arrived, besides[step])
        whole = whole[:half].astype(jnp.float32) + arrived.astype(jnp.float32)
    return whole


def pair_sum(four):
    return (four[0] + four[1]) + (four[2] + four[3])


def absolute(relative, index):
    odd = (index & 1) == 1
    high = (index & 2) == 2
    step = [jnp.where(odd, relative[i ^ 1], relative[i]) for i in range(4)]
    return [jnp.where(high, step[i ^ 2], step[i]) for i in range(4)]


def across(value, axes, split, concat):
    return lax.all_to_all(value, axes, split, concat, tiled=True)


def contract(left, right, left_dim, right_dim):
    return lax.dot_general(
        left,
        right,
        (((left_dim,), (right_dim,)), ((), ())),
        preferred_element_type=jnp.float32,
    )


def turn(block, cosine, sine):
    a, b, c, d = block[0:16], block[16:32], block[32:48], block[48:64]
    cr, cc = cosine[0:16], cosine[16:32]
    sr, sc = sine[0:16], sine[16:32]
    return jnp.concatenate(
        [a * cr - b * sr, a * sr + b * cr, c * cc - d * sc, c * sc + d * cc], axis=0
    )


def unit_of(raw):
    inverse = lax.rsqrt(jnp.mean(raw * raw, axis=0, keepdims=True) + EPSILON)
    return raw * inverse, inverse


def unit_back(incoming, unit, inverse, gain):
    lifted = incoming * gain
    gain_part = jnp.sum(incoming * unit, axis=1, keepdims=True)
    raw_part = inverse * (lifted - unit * jnp.mean(lifted * unit, axis=0, keepdims=True))
    return raw_part, gain_part


QBLOCK = 256
VMEM_LIMIT = 56 * 1024 * 1024


def lanes_of(ref):
    return jnp.concatenate([ref[i] for i in range(PLANE)], axis=-1)


def text_of(ref, kind):
    part = ref.shape[-1] // 2
    lanes = slice(kind * part, (kind + 1) * part)
    return jnp.concatenate([ref[i, :, lanes] for i in range(PLANE)], axis=-1)


def attend_kernel(
    spot_ref,
    q_ref,
    k_ref,
    v_ref,
    text_ref,
    norm_ref,
    cos_ref,
    sin_ref,
    valid_ref,
    gate_ref,
    comb_ref,
    self_ref,
    cross_ref,
    qlow_ref,
    klow_ref,
    tlow_ref,
    rinv_ref,
):
    cosine, sine, valid = cos_ref[...], sin_ref[...], valid_ref[...]
    query = turn(unit_of(q_ref[...])[0] * norm_ref[:, 0:1], cosine, sine).astype(jnp.bfloat16)
    key = turn(unit_of(k_ref[...])[0] * norm_ref[:, 1:2], cosine, sine)
    qlow_ref[...] = query
    klow_ref[...] = key.astype(jnp.bfloat16)
    key_rows = key.T.astype(jnp.bfloat16)
    text_key = unit_of(text_of(text_ref, 0))[0] * norm_ref[:, 2:3]
    tlow_ref[...] = text_key.astype(jnp.bfloat16)
    text_rows = text_key.T.astype(jnp.bfloat16)
    value = v_ref[...].astype(jnp.bfloat16).astype(jnp.float32) * valid
    lanes = value.shape[1]
    value_ones = jnp.concatenate(
        [value, jnp.broadcast_to(valid, (16, lanes))], axis=0
    ).astype(jnp.bfloat16)
    tvalue = text_of(text_ref, 1)
    tvalue_ones = jnp.concatenate(
        [tvalue, jnp.ones((16, tvalue.shape[1]), jnp.float32)], axis=0
    ).astype(jnp.bfloat16)
    gate = gate_ref[0:1, 0:1]
    scaled = (query.astype(jnp.float32) * 0.125).astype(jnp.bfloat16)
    for chunk in range(lanes // QBLOCK):
        cols = slice(chunk * QBLOCK, (chunk + 1) * QBLOCK)
        weight = jnp.exp(contract(key_rows, scaled[:, cols], 1, 0)).astype(jnp.bfloat16)
        total = contract(value_ones, weight, 1, 0)
        rinv = 1.0 / total[64:65]
        own = total[:64] * rinv
        tweight = jnp.exp(contract(text_rows, scaled[:, cols], 1, 0)).astype(jnp.bfloat16)
        ttotal = contract(tvalue_ones, tweight, 1, 0)
        trinv = 1.0 / ttotal[64:65]
        text = ttotal[:64] * trinv
        self_ref[:, cols] = own
        cross_ref[:, cols] = text
        rinv_ref[0:1, cols] = rinv
        rinv_ref[1:2, cols] = trinv
        comb_ref[chunk] = (own + gate * text).astype(jnp.bfloat16)


def attend_back_kernel(
    spot_ref,
    q_ref,
    k_ref,
    v_ref,
    text_ref,
    norm_ref,
    cos_ref,
    sin_ref,
    valid_ref,
    gate_ref,
    self_ref,
    cross_ref,
    qlow_ref,
    klow_ref,
    tlow_ref,
    rinv_ref,
    dcomb_ref,
    dqkv_ref,
    dtext_ref,
    gains_ref,
):
    cosine, sine, valid = cos_ref[...], sin_ref[...], valid_ref[...]
    lanes = valid.shape[1]
    gate = gate_ref[0:1, 0:1]
    dcomb = lanes_of(dcomb_ref).astype(jnp.float32)
    cross = cross_ref[...]
    dself = dcomb.astype(jnp.bfloat16)
    dcross = (dcomb * gate).astype(jnp.bfloat16)
    delta = jnp.sum(dself.astype(jnp.float32) * self_ref[...], axis=0, keepdims=True)
    tdelta = jnp.sum(dcross.astype(jnp.float32) * cross, axis=0, keepdims=True)
    gate_part = jnp.sum(
        jnp.sum(dcomb * cross, axis=0, keepdims=True), axis=1, keepdims=True
    ) * (1.0 - gate * gate)
    query = qlow_ref[...]
    scaled = (query.astype(jnp.float32) * 0.125).astype(jnp.bfloat16)
    key = klow_ref[...].astype(jnp.float32)
    key_rows = key.T.astype(jnp.bfloat16)
    key_held = (key * valid * 0.125).astype(jnp.bfloat16)
    value_rows = v_ref[...].T.astype(jnp.bfloat16)
    text_key = tlow_ref[...].astype(jnp.float32)
    text_rows = text_key.T.astype(jnp.bfloat16)
    text_held = (text_key * 0.125).astype(jnp.bfloat16)
    tvalue_rows = text_of(text_ref, 1).T.astype(jnp.bfloat16)
    dkey = dvalue = dtkey = dtvalue = 0.0
    dquery = []
    for start in range(0, lanes, QBLOCK):
        cols = slice(start, start + QBLOCK)
        probs = jnp.exp(contract(key_rows, scaled[:, cols], 1, 0)) * rinv_ref[0:1, cols]
        dprobs = contract(value_rows, dself[:, cols], 1, 0)
        dscore = (probs * (dprobs - delta[:, cols])).astype(jnp.bfloat16)
        dvalue += contract(dself[:, cols], probs.astype(jnp.bfloat16), 1, 1)
        dkey += contract(scaled[:, cols], dscore, 1, 1)
        turned = contract(key_held, dscore, 1, 0)
        tprobs = jnp.exp(contract(text_rows, scaled[:, cols], 1, 0)) * rinv_ref[1:2, cols]
        dtprobs = contract(tvalue_rows, dcross[:, cols], 1, 0)
        dtscore = (tprobs * (dtprobs - tdelta[:, cols])).astype(jnp.bfloat16)
        dtvalue += contract(dcross[:, cols], tprobs.astype(jnp.bfloat16), 1, 1)
        dtkey += contract(scaled[:, cols], dtscore, 1, 1)
        dquery.append(turned + contract(text_held, dtscore, 1, 0))
    dquery = jnp.concatenate(dquery, axis=1)
    unit, inverse = unit_of(q_ref[...])
    draw_q, query_gain = unit_back(turn(dquery, cosine, -sine), unit, inverse, norm_ref[:, 0:1])
    unit, inverse = unit_of(k_ref[...])
    draw_k, key_gain = unit_back(turn(dkey * valid, cosine, -sine), unit, inverse, norm_ref[:, 1:2])
    unit, inverse = unit_of(text_of(text_ref, 0))
    draw_t, text_gain = unit_back(dtkey, unit, inverse, norm_ref[:, 2:3])
    dvalue = dvalue * valid
    for chunk in range(PLANE):
        cols = slice(chunk * QBLOCK, (chunk + 1) * QBLOCK)
        dqkv_ref[chunk, 0:64] = draw_q[:, cols].astype(jnp.bfloat16)
        dqkv_ref[chunk, 64:128] = draw_k[:, cols].astype(jnp.bfloat16)
        dqkv_ref[chunk, 128:192] = dvalue[:, cols].astype(jnp.bfloat16)
        size = draw_t.shape[1] // PLANE
        cols = slice(chunk * size, (chunk + 1) * size)
        dtext_ref[chunk] = jnp.concatenate([draw_t[:, cols], dtvalue[:, cols]], axis=1).astype(
            jnp.bfloat16
        )
    gains_ref[:, 0:128] = jnp.broadcast_to(query_gain, (64, 128))
    gains_ref[:, 128:256] = jnp.broadcast_to(key_gain, (64, 128))
    gains_ref[:, 256:384] = jnp.broadcast_to(text_gain, (64, 128))
    gains_ref[:, 384:512] = jnp.broadcast_to(gate_part, (64, 128))


def head_block(width, offset=0):
    return pl.BlockSpec((HDIM, width), lambda h, s: (h + offset, 0))


def shared_block(rows, width):
    return pl.BlockSpec((rows, width), lambda h, s: (0, 0))


def params():
    return pltpu.CompilerParams(vmem_limit_bytes=VMEM_LIMIT)


def cost(flops, moved):
    return pl.CostEstimate(flops=flops, bytes_accessed=moved, transcendentals=0)


def attention_call(heads, lanes, texts, backward):
    f32, b16 = jnp.float32, jnp.bfloat16
    part = texts // PLANE
    specs = [
        head_block(lanes),
        head_block(lanes, heads),
        head_block(lanes, 2 * heads),
        pl.BlockSpec((PLANE, HDIM, 2 * part), lambda h, s: (0, h, 0)),
        pl.BlockSpec((HDIM, 3), lambda h, s: (s[0] * heads + h, 0)),
        shared_block(32, lanes),
        shared_block(32, lanes),
        shared_block(1, lanes),
        pl.BlockSpec((8, 128), lambda h, s: (s[0] * heads + h, 0)),
    ]
    wide = heads * HDIM
    chunk_spec = pl.BlockSpec((PLANE, HDIM, QBLOCK), lambda h, s: (0, h, 0))
    rinv_spec = pl.BlockSpec((8, lanes), lambda h, s: (h, 0))
    saved = [head_block(lanes)] * 4 + [head_block(texts), rinv_spec]
    shape = jax.ShapeDtypeStruct
    pairs = heads * lanes * (lanes + texts)
    if not backward:
        out_specs = [chunk_spec] + saved
        out_shape = [
            shape((PLANE, wide, lanes // PLANE), b16),
            shape((wide, lanes), f32),
            shape((wide, lanes), f32),
            shape((wide, lanes), b16),
            shape((wide, lanes), b16),
            shape((wide, texts), b16),
            shape((heads * 8, lanes), f32),
        ]
        body, passes = attend_kernel, 2
    else:
        specs = specs + saved + [chunk_spec]
        out_specs = [
            pl.BlockSpec((PLANE, 3 * HDIM, QBLOCK), lambda h, s: (0, h, 0)),
            pl.BlockSpec((PLANE, HDIM, 2 * part), lambda h, s: (0, h, 0)),
            head_block(512),
        ]
        out_shape = [
            shape((PLANE, 3 * wide, lanes // PLANE), b16),
            shape((PLANE, wide, 2 * part), b16),
            shape((wide, 512), f32),
        ]
        body, passes = attend_back_kernel, 5
    return pl.pallas_call(
        body,
        grid_spec=pltpu.PrefetchScalarGridSpec(
            num_scalar_prefetch=1, grid=(heads,), in_specs=specs, out_specs=out_specs
        ),
        out_shape=out_shape,
        compiler_params=params(),
        cost_estimate=cost(8 * pairs * HDIM * passes, 8 * wide * lanes),
    )


def project_kernel(spot_ref, own_ref, other_ref, lift_ref, weight_ref, in_ref, qkv_ref, turned):
    @pl.when(pl.program_id(0) == 0)
    def _():
        turned[...] = weight_ref[...].T

    first = spot_ref[1] == 0
    own, other = own_ref[...].astype(jnp.float32), other_ref[...].astype(jnp.float32)
    values = jnp.concatenate([jnp.where(first, own, other), jnp.where(first, other, own)])
    normed = (values * rms_inverse(values) * lift_ref[...]).astype(jnp.bfloat16)
    in_ref[...] = normed
    qkv_ref[...] = contract(turned[...], normed, 1, 1)


def project(spot, halves, lift, weight):
    rows, width = halves[0].shape
    wide = weight.shape[1]
    block = rows // PLANE
    return pl.pallas_call(
        project_kernel,
        grid_spec=pltpu.PrefetchScalarGridSpec(
            num_scalar_prefetch=1,
            grid=(PLANE,),
            in_specs=[
                pl.BlockSpec((block, width), lambda i, s: (i, 0)),
                pl.BlockSpec((block, width), lambda i, s: (i % 2 * 2 + i // 2, 0)),
                pl.BlockSpec((1, width), lambda i, s: (0, 0)),
                pl.BlockSpec((width, wide), lambda i, s: (0, 0)),
            ],
            out_specs=[
                pl.BlockSpec((2 * block, width), lambda i, s: (s[2 + i] // 2, 0)),
                pl.BlockSpec((wide, 2 * block), lambda i, s: (0, s[2 + i] // 2)),
            ],
            scratch_shapes=[pltpu.VMEM((wide, width), jnp.bfloat16)],
        ),
        out_shape=[
            jax.ShapeDtypeStruct((2 * rows, width), jnp.bfloat16),
            jax.ShapeDtypeStruct((wide, 2 * rows), jnp.float32),
        ],
        compiler_params=params(),
        cost_estimate=cost(4 * rows * width * wide, 16 * rows * width),
    )(spot, *halves, lift, weight)


def ffn_kernel(spot_ref, a_ref, b_ref, d0_ref, d1_ref, gw_ref, uw_ref, dw_ref, h_ref, din_ref):
    early = pl.program_id(0) < 2
    rows_in = jnp.where(early, a_ref[...], b_ref[...])
    d_out = jnp.concatenate([d0_ref[...], d1_ref[...]])
    size = gw_ref.shape[1]
    gate_pre = jnp.dot(rows_in, gw_ref[...], preferred_element_type=jnp.float32)
    up_pre = jnp.dot(rows_in, uw_ref[...], preferred_element_type=jnp.float32)
    d_hidden = contract(d_out, dw_ref[...], 1, 1)
    gate_sig = jax.nn.sigmoid(gate_pre)
    swish = gate_pre * gate_sig
    d_gate = (d_hidden * up_pre * (gate_sig + swish * (1.0 - gate_sig))).astype(jnp.bfloat16)
    d_up = (d_hidden * swish).astype(jnp.bfloat16)
    h_ref[:, 0:size] = d_gate
    h_ref[:, size : 2 * size] = d_up
    h_ref[:, 2 * size : 3 * size] = (swish * up_pre).astype(jnp.bfloat16)
    din_ref[...] = (
        contract(d_gate, gw_ref[...], 1, 1) + contract(d_up, uw_ref[...], 1, 1)
    ).astype(jnp.bfloat16)


def ffn(spot, halves, d_ffn, gate_weight, up_weight, down_weight):
    rows, width = halves[0].shape
    size = gate_weight.shape[1] // PLANE
    block = rows // 2
    early = pl.BlockSpec((block, width), lambda i, s: (jnp.minimum(i, 1), 0))
    late = pl.BlockSpec((block, width), lambda i, s: (jnp.maximum(i - 2, 0), 0))
    col = pl.BlockSpec((width, size), lambda i, s: (0, s[0]))
    return pl.pallas_call(
        ffn_kernel,
        grid_spec=pltpu.PrefetchScalarGridSpec(
            num_scalar_prefetch=1,
            grid=(4,),
            in_specs=[
                early,
                late,
                pl.BlockSpec((block // 2, width), lambda i, s: (s[2 + 2 * i], 0)),
                pl.BlockSpec((block // 2, width), lambda i, s: (s[3 + 2 * i], 0)),
                col,
                col,
                pl.BlockSpec((size, width), lambda i, s: (s[0], 0)),
            ],
            out_specs=[
                pl.BlockSpec((block, 3 * size), lambda i, s: (i, 0)),
                pl.BlockSpec((block, width), lambda i, s: (i, 0)),
            ],
        ),
        out_shape=[
            jax.ShapeDtypeStruct((2 * rows, 3 * size), jnp.bfloat16),
            jax.ShapeDtypeStruct((2 * rows, width), jnp.bfloat16),
        ],
        compiler_params=params(),
        cost_estimate=cost(20 * rows * width * size, 16 * rows * width),
    )(spot, *halves, d_ffn, d_ffn, gate_weight, up_weight, down_weight)


def ffn_grad_kernel(
    spot_ref, a_ref, b_ref, d_ref, inner_ref, hid_ref, dw_ref, grad_ref, out_ref
):
    rows = a_ref.shape[0]
    size = hid_ref.shape[1]
    block = rows // 4
    starts = [pl.multiple_of(spot_ref[2 + i] * block, block) for i in range(8)]
    d_rows = jnp.concatenate([d_ref[pl.ds(start, block), :] for start in starts])
    in_rows = jnp.concatenate([a_ref[...], b_ref[...]])
    hidden = hid_ref[...]
    grad_ref[:, : 2 * size] = contract(in_rows, inner_ref[...], 0, 0).astype(jnp.bfloat16)
    grad_ref[:, 2 * size :] = contract(d_rows, hidden, 0, 0).astype(jnp.bfloat16)
    out_ref[...] = jnp.dot(hidden, dw_ref[...], preferred_element_type=jnp.float32).astype(
        jnp.bfloat16
    )


def ffn_grad(spot, halves, d_ffn, inner, down_weight):
    rows, width = halves[0].shape
    size = inner.shape[1] // 3
    tile = width // 3
    return pl.pallas_call(
        ffn_grad_kernel,
        grid_spec=pltpu.PrefetchScalarGridSpec(
            num_scalar_prefetch=1,
            grid=(3,),
            in_specs=[
                pl.BlockSpec((rows, tile), lambda i, s: (0, i)),
                pl.BlockSpec((rows, tile), lambda i, s: (0, i)),
                pl.BlockSpec((2 * rows, tile), lambda i, s: (0, i)),
                pl.BlockSpec((2 * rows, 2 * size), lambda i, s: (0, 0)),
                pl.BlockSpec((2 * rows, size), lambda i, s: (0, 2)),
                pl.BlockSpec((size, tile), lambda i, s: (s[0], i)),
            ],
            out_specs=[
                pl.BlockSpec((tile, 3 * size), lambda i, s: (i, 0)),
                pl.BlockSpec((2 * rows, tile), lambda i, s: (0, i)),
            ],
        ),
        out_shape=[
            jax.ShapeDtypeStruct((width, 3 * size), jnp.bfloat16),
            jax.ShapeDtypeStruct((2 * rows, width), jnp.bfloat16),
        ],
        compiler_params=params(),
        cost_estimate=cost(16 * rows * width * size, 16 * rows * width),
    )(spot, *halves, d_ffn, inner, inner, down_weight)


def by_kind(block, kind, heads):
    return jnp.concatenate(
        [
            block[i, (3 * h + kind) * HDIM : (3 * h + kind + 1) * HDIM]
            for i in range(block.shape[0])
            for h in range(heads)
        ],
        axis=0,
    )


def input_grad_kernel(d_ref, qw_ref, kw_ref, vw_ref, out_ref):
    heads = d_ref.shape[1] // (3 * HDIM)
    total = 0.0
    for kind, weight in enumerate((qw_ref, kw_ref, vw_ref)):
        total += contract(by_kind(d_ref, kind, heads).T, weight[...], 1, 1)
    out_ref[...] = total


def input_grad(d_qkv, query_weight, key_weight, value_weight):
    width, wide = query_weight.shape
    rows = d_qkv.shape[2]
    tile = width // 3
    weight = pl.BlockSpec((tile, wide), lambda i: (i, 0))
    return pl.pallas_call(
        input_grad_kernel,
        grid=(3,),
        in_specs=[pl.BlockSpec(d_qkv.shape, lambda i: (0, 0, 0)), weight, weight, weight],
        out_specs=pl.BlockSpec((rows, tile), lambda i: (0, i)),
        out_shape=jax.ShapeDtypeStruct((rows, width), jnp.float32),
        compiler_params=params(),
        cost_estimate=cost(6 * rows * width * wide, 6 * width * wide),
    )(d_qkv, query_weight, key_weight, value_weight)


def attn_grad_kernel(spot_ref, in_ref, own_ref, other_ref, d_ref, comb_ref, out_ref):
    places, _, rows = d_ref.shape
    wide = comb_ref.shape[1]
    heads = wide // HDIM
    first = spot_ref[1] == 0
    total = branch = 0.0
    for place in range(places):
        part = slice(place * rows, (place + 1) * rows)
        block = d_ref[place : place + 1]
        ordered = jnp.concatenate([by_kind(block, kind, heads) for kind in range(3)])
        total += contract(in_ref[part].T, ordered, 1, 1)
        own, other = own_ref[place], other_ref[place]
        d_attn = jnp.concatenate([jnp.where(first, own, other), jnp.where(first, other, own)])
        branch += contract(d_attn.T, comb_ref[place], 1, 1)
    out_ref[:, : 3 * wide] = total.astype(jnp.bfloat16)
    out_ref[:, 3 * wide :] = branch.astype(jnp.bfloat16)


def attn_grad(spot, attn_in, own_d_attn, other_d_attn, d_qkv, combined):
    rows, width = attn_in.shape
    wide = combined.shape[1]
    tile = width // 3
    core_rows = pl.BlockSpec(own_d_attn.shape[:2] + (tile,), lambda i, s: (0, 0, i))
    return pl.pallas_call(
        attn_grad_kernel,
        grid_spec=pltpu.PrefetchScalarGridSpec(
            num_scalar_prefetch=1,
            grid=(3,),
            in_specs=[
                pl.BlockSpec((rows, tile), lambda i, s: (0, i)),
                core_rows,
                core_rows,
                pl.BlockSpec(d_qkv.shape, lambda i, s: (0, 0, 0)),
                pl.BlockSpec(combined.shape, lambda i, s: (0, 0, 0)),
            ],
            out_specs=pl.BlockSpec((tile, 4 * wide), lambda i, s: (i, 0)),
        ),
        out_shape=jax.ShapeDtypeStruct((width, 4 * wide), jnp.bfloat16),
        compiler_params=params(),
        cost_estimate=cost(8 * rows * width * wide, 4 * rows * width),
    )(spot, attn_in, own_d_attn, other_d_attn, d_qkv, combined)


def strips_kernel(in_ref, out_ref):
    size = out_ref.shape[2]
    for strip in range(out_ref.shape[0]):
        out_ref[strip] = in_ref[:, strip * size : (strip + 1) * size]


def by_strips(states):
    rows, cols = states.shape
    return pl.pallas_call(
        strips_kernel,
        out_shape=jax.ShapeDtypeStruct((STRIPS, rows, cols // STRIPS), states.dtype),
        compiler_params=params(),
        cost_estimate=cost(0, 4 * rows * cols),
    )(states)


def text_grad_kernel(where_ref, *refs):
    states, d_text, out_ref = refs[:PLANE], refs[PLANE : 2 * PLANE], refs[2 * PLANE]
    own = where_ref[1]
    part = d_text[0].shape[2] // 2
    total = 0.0
    for mask in range(PLANE):
        place = where_ref[0] ^ mask
        blocks = [
            jnp.concatenate([piece[place, :, :part], piece[place, :, part:]]) for piece in d_text
        ]
        rows = [
            states[mask][pl.ds(pl.multiple_of((own ^ strip) * part, part), part), :]
            for strip in range(STRIPS)
        ]
        total += jnp.dot(
            jnp.concatenate(blocks, axis=-1),
            jnp.concatenate(rows),
            preferred_element_type=jnp.float32,
        )
    size = total.shape[1] // PLANE
    for place in range(PLANE):
        out_ref[place] = total[:, place * size : (place + 1) * size].astype(jnp.bfloat16)


def text_weight_grad(where_here, states, strips):
    rows, cols = states[0].shape
    wide = 2 * strips[0].shape[1]
    whole = pl.BlockSpec(memory_space=pltpu.VMEM)
    return pl.pallas_call(
        text_grad_kernel,
        in_specs=[pl.BlockSpec(memory_space=pltpu.SMEM)] + [whole] * 8,
        out_specs=whole,
        out_shape=jax.ShapeDtypeStruct((PLANE, wide, cols // PLANE), jnp.bfloat16),
        compiler_params=params(),
        cost_estimate=cost(8 * rows * cols * wide, 8 * rows * cols),
    )(where_here, *states, *strips)


def split_three(value):
    high = lax.reduce_precision(value, 8, 7)
    middle = lax.reduce_precision(value - high, 8, 7)
    return jnp.concatenate([high, middle, value - high - middle]).astype(jnp.bfloat16)


def strip_shards(
    tokens,
    cotangent,
    step_embed,
    item_band,
    item_length,
    item_width,
    text_states,
    ada_weight,
    ada_bias,
    attn_gain,
    ffn_gain,
    query_weight,
    key_weight,
    value_weight,
    query_gain,
    key_gain,
    cross_gate,
    text_key_weight,
    text_value_weight,
    text_key_gain,
    out_weight,
    gate_weight,
    up_weight,
    down_weight,
):
    f32, b16 = jnp.float32, jnp.bfloat16
    strip = lax.axis_index("z")
    place = lax.axis_index("y") * 2 + lax.axis_index("x")
    core = lax.axis_index("c")
    first_core = core == 0
    spot = [place, core]
    for block in range(2 * PLANE):
        from_core = core ^ (block // PLANE)
        from_place = place
        if block & 1:
            from_place = from_place ^ (1 + from_core)
        if block & 2:
            from_place = from_place ^ (2 - from_core)
        spot.append(from_place * CORES + from_core)
    spot = jnp.stack(spot).astype(jnp.int32)
    width = tokens.shape[1]
    half = SLOT // CORES
    own_rows = STRIPS * half
    lanes = own_rows * PLANE * CORES
    wide = query_weight.shape[1] // PLANE
    heads = wide // HDIM
    hidden_wide = gate_weight.shape[1] // PLANE
    text_own = text_states.shape[0]
    texts = text_own * PLANE

    def both_cores(own, axis=0):
        other = move(own, FLIP_CORE)
        low = jnp.where(first_core, own, other)
        high = jnp.where(first_core, other, own)
        return jnp.concatenate([low, high], axis=axis)

    def core_scatter(partial, axis=0):
        size = partial.shape[axis] // CORES
        sent = lax.dynamic_slice_in_dim(partial, (1 - core) * size, size, axis)
        kept = lax.dynamic_slice_in_dim(partial, core * size, size, axis)
        return kept.astype(f32) + move(sent.astype(b16), FLIP_CORE).astype(f32)

    def to_items(*arrays):
        parts = [
            lax.dynamic_slice_in_dim(a.reshape(ITEMS, SLOT, width), core * half, half, 1)
            for a in arrays
        ]
        parts = across(jnp.concatenate(parts, axis=1), "z", 0, 0)
        parts = parts.reshape(STRIPS, len(arrays), half, width)
        return [parts[:, i].reshape(own_rows, width) for i in range(len(arrays))]

    def from_items(beside, *arrays):
        parts = jnp.concatenate([a.reshape(STRIPS, half, width) for a in arrays], axis=1)
        parts = across(parts, "z", 0, 0)
        other = move(after(parts, beside), FLIP_CORE)
        outs = []
        for i in range(len(arrays)):
            own_part, other_part = (p[:, i * half : (i + 1) * half] for p in (parts, other))
            low = jnp.where(first_core, own_part, other_part)
            high = jnp.where(first_core, other_part, own_part)
            outs.append(jnp.concatenate([low, high], axis=1).reshape(ITEMS * SLOT, width))
        return outs

    own_tokens, incoming_low = to_items(tokens, cotangent)
    text_raw = jnp.concatenate(
        [
            contract(text_key_weight, text_states, 0, 1),
            contract(text_value_weight, text_states, 0, 1).astype(b16).astype(f32),
        ],
        axis=1,
    ).reshape(PLANE, wide, 2 * text_own)
    qkv_weight = jnp.concatenate(
        [
            lax.dynamic_slice_in_dim(weight, place * wide, wide, 1)
            for weight in (query_weight, key_weight, value_weight)
        ],
        axis=1,
    )
    silu_embed = jax.nn.silu(step_embed.astype(f32))
    products = jnp.dot(split_three(silu_embed), ada_weight, preferred_element_type=f32)
    local_mod = products[0:4] + products[4:8] + products[8:12] + ada_bias
    own_tokens = after(own_tokens, text_raw, qkv_weight, local_mod)
    pair = jnp.concatenate([own_tokens, move(own_tokens, FLIP_FIRST)])
    pair_arrived = move(pair, FLIP_SECOND)
    text_raw = across(after(text_raw, pair), PLANE_AXES, 0, 0)

    other_mod = move(after(local_mod, own_tokens), FLIP_CORE)
    low_mod = jnp.where(first_core, local_mod, other_mod)
    high_mod = jnp.where(first_core, other_mod, local_mod)

    item_ids = jnp.arange(ITEMS, dtype=jnp.int32)
    band_mask = (item_band[:, None] == item_ids[None, :]).astype(f32)
    own_mask = jnp.sum(jnp.where(item_ids[:, None] == strip, band_mask, 0.0), axis=0)

    own_low = jnp.sum(own_mask[:, None] * low_mod, axis=0)
    own_high = jnp.sum(own_mask[:, None] * high_mod, axis=0)
    scale_attn, scale_ffn = own_low[:width], own_high[:width]
    lift_attn = attn_gain * (1.0 + scale_attn)
    lift_ffn = ffn_gain * (1.0 + scale_ffn)
    gate_attn = jnp.tanh(own_low[width:])
    gate_ffn = jnp.tanh(own_high[width:])

    lane = jnp.arange(lanes, dtype=jnp.int32)
    from_place = lane // (own_rows * CORES)
    from_core = (lane // own_rows) % CORES
    from_strip = (lane % own_rows) // half
    position = (from_strip * PLANE + from_place) * SLOT + from_core * half + lane % half
    chosen = jnp.where(item_ids[:, None] == strip, 1, 0)
    width_here = jnp.sum(chosen * after(item_width, pair)[:, None], axis=0)
    length_here = jnp.sum(chosen * item_length[:, None], axis=0)
    grid_row = (position // width_here).astype(f32)
    grid_col = (position % width_here).astype(f32)
    quarter = HDIM // 4
    frequency = ROPE_BASE ** (-jnp.arange(quarter, dtype=f32) / quarter)
    angles = jnp.concatenate(
        [frequency[:, None] * grid_row[None, :], frequency[:, None] * grid_col[None, :]]
    )
    cosine, sine = jnp.cos(angles), jnp.sin(angles)
    valid = (position < length_here).astype(f32)[None, :]

    norm_gains = jnp.stack([query_gain, key_gain, text_key_gain], axis=1)
    gate_tiles = jnp.broadcast_to(jnp.tanh(cross_gate)[:, None, None], (cross_gate.shape[0], 8, 128))
    gate_tiles = gate_tiles.reshape(-1, 128)

    low_half = jnp.concatenate(
        [pair, after(pair_arrived, lift_attn, text_raw, cosine, sine, norm_gains, gate_tiles)]
    )
    incoming = after(incoming_low, pair).astype(f32)
    own_d_ffn = (gate_ffn * incoming).astype(b16)
    high_half = after(move(low_half, FLIP_CORE), own_d_ffn)
    d_ffn = lax.all_gather(after(own_d_ffn, low_half), PLANE_AXES + ("c",), axis=0, tiled=True)
    attn_in, qkv = project(spot, (low_half, high_half), lift_attn[None, :], qkv_weight)
    common = (
        spot,
        qkv,
        qkv,
        qkv,
        text_raw,
        norm_gains,
        cosine,
        sine,
        valid,
        gate_tiles,
    )
    combined, *saved = attention_call(heads, lanes, texts, False)(*common)
    chip_combined = across(combined, PLANE_AXES, 0, 0).reshape(-1, own_rows * CORES)
    attn_branch = core_scatter(contract(chip_combined, out_weight, 0, 0))

    residual = own_tokens.astype(f32)
    middle = residual + gate_attn * attn_branch
    inverse_two = rms_inverse(middle)
    normed_two = middle * inverse_two
    own_ffn_in = (normed_two * lift_ffn).astype(b16)
    own_ffn_in = after(own_ffn_in, d_ffn)
    states_wide = text_states.shape[1] // STRIPS
    states = by_strips(after(text_states, own_ffn_in))
    states = across(states, "z", 0, 0).reshape(texts, states_wide)
    ffn_in = plane_gather(own_ffn_in, (states,))
    inner, d_ffn_in = ffn(spot, ffn_in, d_ffn, gate_weight, up_weight, down_weight)
    ffn_grads, ffn_branch = ffn_grad(spot, ffn_in, d_ffn, inner, down_weight)
    branch_half = core_half(ffn_branch)
    d_ffn_in = plane_scatter(d_ffn_in, (ffn_grads,), (branch_half,))
    d_normed = d_ffn_in * normed_two
    u_ffn = jnp.sum(d_normed, axis=0)
    d_middle = incoming + inverse_two * (
        d_ffn_in * lift_ffn
        - normed_two * jnp.mean(d_normed * lift_ffn, axis=-1, keepdims=True)
    )
    w_attn = jnp.sum(d_middle * attn_branch, axis=0) * (1.0 - gate_attn * gate_attn)
    own_d_attn = (gate_attn * d_middle).astype(b16)
    d_attn = both_cores(own_d_attn)

    d_comb = contract(out_weight, d_attn, 1, 1).astype(b16).reshape(PLANE, wide, -1)
    d_comb = across(d_comb, PLANE_AXES, 0, 0)
    d_qkv, d_text, gains = attention_call(heads, lanes, texts, True)(*common, *saved, d_comb)
    own_rows_d = jnp.broadcast_to(after(own_d_attn, d_comb), (PLANE, own_rows, width))
    own_rows_d = across(own_rows_d, PLANE_AXES, 0, 0)
    own_rows_d = after(own_rows_d, d_qkv)
    attn_grads = attn_grad(spot, attn_in, own_rows_d, move(own_rows_d, FLIP_CORE), d_qkv, combined)
    chip_d_qkv = after(across(d_qkv, PLANE_AXES, 0, 0), attn_grads)
    ffn_branch = plane_scatter(after(branch_half, chip_d_qkv))
    d_attn_in = core_scatter(input_grad(chip_d_qkv, query_weight, key_weight, value_weight))
    inverse_one = rms_inverse(residual)
    normed_one = residual * inverse_one
    d_normed = d_attn_in * normed_one
    u_attn = jnp.sum(d_normed, axis=0)
    tokens_grad = d_middle + inverse_one * (
        d_attn_in * lift_attn
        - normed_one * jnp.mean(d_normed * lift_attn, axis=-1, keepdims=True)
    )

    w_ffn = jnp.sum(incoming * ffn_branch, axis=0) * (1.0 - gate_ffn * gate_ffn)
    block_out = (middle + gate_ffn * ffn_branch).astype(b16)

    def spread(own):
        blocks = own.reshape(PLANE, own.shape[0] // PLANE, own.shape[1])
        return across(blocks, PLANE_AXES, 0, 0)

    def sheet(blocks, start, size):
        return jnp.concatenate(
            [blocks[i, :, start : start + size] for i in range(PLANE)], axis=1
        ).astype(f32)

    ffn_own = lax.psum_scatter(ffn_grads, "z", scatter_dimension=0, tiled=True)
    d_text_all = gather_by(d_text, FLIP_STRIP)
    attn_grads = lax.psum_scatter(after(attn_grads, ffn_own, d_text_all), "z", scatter_dimension=0, tiled=True)
    ffn_blocks = spread(ffn_own)
    attn_blocks = spread(attn_grads)
    block_out, tokens_grad = from_items(ffn_blocks, block_out, tokens_grad.astype(b16))
    gate_grad = sheet(ffn_blocks, 0, hidden_wide)
    up_grad = sheet(ffn_blocks, hidden_wide, hidden_wide)
    down_grad = sheet(ffn_blocks, 2 * hidden_wide, hidden_wide).T
    out_grad = sheet(attn_blocks, 3 * wide, wide).T
    query_grad = sheet(attn_blocks, 0, wide)
    key_grad = sheet(attn_blocks, wide, wide)
    value_grad = sheet(attn_blocks, 2 * wide, wide)

    back = across(after(d_text, chip_d_qkv), PLANE_AXES, 0, 0)
    back = after(back, attn_grads).reshape(-1, 2 * text_own)
    back = [back[:, :text_own], back[:, text_own:]]
    text_grad = core_scatter(
        contract(back[0], text_key_weight, 0, 1) + contract(back[1], text_value_weight, 0, 1), 1
    )
    states = gather_by(after(states, d_qkv), FLIP_PLACE)
    where_here = jnp.stack([place, strip]).astype(jnp.int32)
    states[0] = after(states[0], ffn_blocks)
    text_sum = text_weight_grad(where_here, states, d_text_all)
    text_blocks = across(text_sum, PLANE_AXES, 0, 0)
    text_key_grad = text_blocks[:, :wide].reshape(PLANE * wide, -1).T.astype(f32)
    text_value_grad = text_blocks[:, wide:].reshape(PLANE * wide, -1).T.astype(f32)

    own_sums = jnp.concatenate([u_attn, u_ffn, w_ffn, w_attn])
    own_sums = own_sums + move(own_sums, FLIP_CORE)
    count = own_sums.shape[0]
    parts = jnp.concatenate(
        [own_sums, gains[:, 0], gains[:, 128], gains[:, 256], gains[:, 384]]
    )
    parts = gather_by(parts, FLIP_PLACE)
    head_parts = absolute([p[count:].reshape(4, wide) for p in parts], place)
    parts = jnp.concatenate(
        [pair_sum([p[:count] for p in parts]), jnp.concatenate(head_parts, axis=1).reshape(-1)]
    )
    parts = gather_by(after(parts, attn_grads), FLIP_STRIP)
    head_parts = pair_sum([p[count:] for p in parts]).reshape(4, PLANE * wide)
    sums = [p[:count].reshape(4, width) for p in absolute(parts, strip)]
    items = []
    for item in range(ITEMS):
        low_part = jnp.concatenate([attn_gain * sums[item][0], sums[item][3]])
        high_part = jnp.concatenate([ffn_gain * sums[item][1], sums[item][2]])
        items.append(jnp.where(first_core, low_part, high_part))
    ada_bias_grad = pair_sum(items)
    def by_item(table):
        return jnp.sum(band_mask[:, :, None] * table[None], axis=1)

    scales = by_item(low_mod[:, :width]), by_item(high_mod[:, :width])
    attn_gain_grad = pair_sum([sums[i][0] * (1.0 + scales[0][i]) for i in range(ITEMS)])
    ffn_gain_grad = pair_sum([sums[i][1] * (1.0 + scales[1][i]) for i in range(ITEMS)])
    ada_rows = silu_embed.shape[1] // (STRIPS * PLANE)
    silu_own = lax.dynamic_slice_in_dim(
        silu_embed, (strip * PLANE + place) * ada_rows, ada_rows, 1
    )
    ada_grad = lax.dot_general(
        by_item(silu_own), jnp.stack(items), (((0,), (0,)), ((), ())), precision=HIGHEST
    )
    return (
        block_out,
        tokens_grad,
        text_grad,
        ada_grad,
        ada_bias_grad,
        attn_gain_grad,
        ffn_gain_grad,
        query_grad,
        key_grad,
        value_grad,
        head_parts[0],
        head_parts[1],
        head_parts[3].reshape(-1, HDIM)[:, 0],
        text_key_grad,
        text_value_grad,
        head_parts[2],
        out_grad,
        gate_grad,
        up_grad,
        down_grad,
    )


def placements(seq, tp):
    ins = (
        P(seq, None),
        P(seq, None),
        P(),
        P(),
        P(),
        P(),
        P(seq, None),
        P(None, tp),
        P(tp),
        P(),
        P(),
        P(None, tp),
        P(None, tp),
        P(None, tp),
        P(tp),
        P(tp),
        P(tp),
        P(None, tp),
        P(None, tp),
        P(tp),
        P(tp, None),
        P(None, tp),
        P(None, tp),
        P(tp, None),
    )
    outs = (
        P(seq, None),
        P(seq, None),
        P(seq, tp),
        P(seq, tp),
        P(tp),
        P(),
        P(),
        P(seq, tp),
        P(seq, tp),
        P(seq, tp),
        P(tp),
        P(tp),
        P(tp),
        P(seq, tp),
        P(seq, tp),
        P(tp),
        P(tp, seq),
        P(seq, tp),
        P(seq, tp),
        P(tp, seq),
    )
    return ins, outs


def solution(mesh):
    if mesh.shape["seq"] == STRIPS * PLANE and mesh.shape["tp"] == CORES:
        body, seq, tp = strip_shards, ("z", "y", "x"), "c"
        mesh = Mesh(mesh.devices.reshape(STRIPS, 2, 2, CORES), MESH_AXES)
    else:
        body, seq, tp = shards, "seq", "tp"
    ins, outs = placements(seq, tp)
    return jax.shard_map(body, mesh=mesh, in_specs=ins, out_specs=outs, check_vma=False)
```

profile of v0, /device:TPU:0, one launch (start us, length us, event | category | flops | bytes accessed | tf_op | source)
XLA Modules:
  0.0 406.9 jit_solution(15779404750361352346)
XLA Ops:
  10.4 6.3 %all-to-all-start = ((bf16[4,64,1536]{2,1,0:T(8,128)(2,1)}), bf16[4,64,1536]{2,1,0:T(8,128)(2,1)}, u32[]{:S(2)}, u32[]{:S(2)}) async-start(bf16[4,64,1536]{2,1,0:T(8,128)(2,1)} %pad_maximum_fusion.1), calls=%async_computation | async-start | bytes 1572864 | tf_op jit(solution)/shard_map/all_to_all | solution.py:542
  72.2 8.4 %shard_map.383 = (bf16[1024,1536]{1,0:T(8,128)(2,1)}, f32[576,1024]{1,0:T(8,128)}) custom-call(s32[10]{0:T(128)} %stack.69.spot_ref, bf16[512,1536]{1,0:T(8,128)(2,1)} %constant_dynamic-update-slice_fusion.2.own_ref, bf16[512,1536]{1,0:T(8,128)(2,1)} %collective-permute-done.3.other_ref, f32[1,1536]{1,0:T(1,128)} %broadcast_in_dim.37.lift_ref, ...), custom_call_target="tpu_custom_call" | custom-call | flops 1811939328 | bytes 12582912 | tf_op jit(solution)/shard_map/pallas_call | solution.py:818
  80.6 11.6 %shard_map.384 = (bf16[4,192,256]{2,1,0:T(8,128)(2,1)}, f32[192,1024]{1,0:T(8,128)}, f32[192,1024]{1,0:T(8,128)}, bf16[192,1024]{1,0:T(8,128)(2,1)}, bf16[192,10...) custom-call(s32[10]{0:T(128)} %stack.69.spot_ref, f32[576,1024]{1,0:T(8,128)} %get-tuple-element.67.q_ref.k_ref.v_ref, ...), custom_call_target="tpu_custom_call" | custom-call | flops 4026531840 | bytes 1572864 | tf_op jit(solution)/shard_map/pallas_call | solution.py:1250
  96.0 8.2 %all-to-all-done.2 = bf16[4,192,256]{2,1,0:T(8,128)(2,1)S(1)} async-done(((bf16[4,192,256]{2,1,0:T(8,128)(2,1)}), bf16[4,192,256]{2,1,0:T(8,128)(2,1)S(1)}, u32[]{:S(2)}, u32[]{:S(2)}) %all-to-all-start.2) | async-done | bytes 393248 | tf_op jit(solution)/shard_map/all_to_all | solution.py:542
  115.6 4.6 %all-to-all-start.3 = ((bf16[4,64,1024]{2,1,0:T(8,128)(2,1)}), bf16[4,64,1024]{2,1,0:T(8,128)(2,1)}, u32[]{:S(2)}, u32[]{:S(2)}) async-start(bf16[4,64,1024]{2,1,0:T(8,128)(2,1)} %shard_map.385), calls=%async_computation.3 | async-start | bytes 1048576 | tf_op jit(solution)/shard_map/all_to_all | solution.py:542
  126.5 8.4 %all-to-all-done.3 = bf16[4,64,1024]{2,1,0:T(8,128)(2,1)} async-done(((bf16[4,64,1024]{2,1,0:T(8,128)(2,1)}), bf16[4,64,1024]{2,1,0:T(8,128)(2,1)}, u32[]{:S(2)}, u32[]{:S(2)}) %all-to-all-start.3) | async-done | bytes 524320 | tf_op jit(solution)/shard_map/all_to_all | solution.py:542
  141.7 14.5 %shard_map.386 = (bf16[1024,1536]{1,0:T(8,128)(2,1)}, bf16[1024,1536]{1,0:T(8,128)(2,1)}) custom-call(s32[10]{0:T(128)} %stack.69.spot_ref, bf16[512,1536]{1,0:T(8,128)(2,1)} %constant_dynamic-update-slice_fusion.5.a_ref, bf16[512,1536]{1,0:T(8,128)(2,1)} %copy-done.68, bf16[1024,1536]{1,0:T(8,128)(2,1)} %all-gather.2.cloned.1.call-done.d0_ref.d1_ref.d_ref, ...), custom_call_target="tpu_custom_call" | custom-call | flops 8053063680 | bytes 12582912 | tf_op jit(solution)/shard_map/pallas_call | solution.py:871
  157.9 11.8 %shard_map.387 = (bf16[1536,1536]{1,0:T(8,128)(2,1)}, bf16[1024,1536]{1,0:T(8,128)(2,1)}) custom-call(s32[10]{0:T(128)} %stack.69.spot_ref, bf16[512,1536]{1,0:T(8,128)(2,1)} %constant_dynamic-update-slice_fusion.5.a_ref, bf16[512,1536]{1,0:T(8,128)(2,1)} %copy-done.68, bf16[1024,1536]{1,0:T(8,128)(2,1)} %all-gather.2.cloned.1.call-done.d0_ref.d1_ref.d_ref, ...), custom_call_target="tpu_custom_call" | custom-call | flops 6442450944 | bytes 12582912 | tf_op jit(solution)/shard_map/pallas_call | solution.py:920
  184.4 6.8 %collective-permute-done.10 = bf16[256,1536]{1,0:T(8,128)(2,1)} collective-permute-done((bf16[256,1536]{1,0:T(8,128)(2,1)}, bf16[256,1536]{1,0:T(8,128)(2,1)}, u32[]{:S(2)}, u32[]{:S(2)}) %collective-permute-start.10) | collective-permute-done | bytes 786464 | tf_op jit(solution)/shard_map/ppermute | solution.py:494
  194.0 6.4 %collective-permute-done.11 = bf16[128,1536]{1,0:T(8,128)(2,1)S(1)} collective-permute-done((bf16[128,1536]{1,0:T(8,128)(2,1)S(1)}, bf16[128,1536]{1,0:T(8,128)(2,1)S(1)}, u32[]{:S(2)}, u32[]{:S(2)}) %collective-permute-start.11) | collective-permute-done | bytes 393248 | tf_op jit(solution)/shard_map/ppermute | solution.py:494
  207.9 10.8 %all_to_all.60.dcomb_ref = bf16[4,192,256]{2,1,0:T(8,128)(2,1)} all-to-all(bf16[4,192,256]{2,1,0:T(8,128)(2,1)S(1)} %bitcast.123), channel_id=1, replica_groups=mesh['z'=4,'y'=2,'x'=2,'c'=2] {'y','x'}, dimensions={0} | all-to-all | bytes 786432 | tf_op jit(solution)/shard_map/all_to_all | solution.py:542
  223.8 15.7 %shard_map.388 = (bf16[4,576,256]{2,1,0:T(8,128)(2,1)}, bf16[4,192,128]{2,1,0:T(8,128)(2,1)}, f32[192,512]{1,0:T(8,128)}) custom-call(s32[10]{0:T(128)} %stack.69.spot_ref, f32[576,1024]{1,0:T(8,128)} %get-tuple-element.67.q_ref.k_ref.v_ref, f32[576,1024]{1,0:T(8,128)} %get-tuple-element.67.q_ref.k_ref.v_ref, ...), custom_call_target="tpu_custom_call" | custom-call | flops 10066329600 | bytes 1572864 | tf_op jit(solution)/shard_map/pallas_call | solution.py:1280
  242.2 4.3 %all-to-all-start.5 = ((bf16[4,576,256]{2,1,0:T(8,128)(2,1)}), bf16[4,576,256]{2,1,0:T(8,128)(2,1)}, u32[]{:S(2)}, u32[]{:S(2)}) async-start(bf16[4,576,256]{2,1,0:T(8,128)(2,1)} %get-tuple-element.85.d_ref), calls=%async_computation.5 | async-start | bytes 2359296 | tf_op jit(solution)/shard_map/all_to_all | solution.py:542
  249.4 8.3 %shard_map.389 = bf16[1536,768]{1,0:T(8,128)(2,1)} custom-call(s32[10]{0:T(128)} %stack.69.spot_ref, bf16[1024,1536]{1,0:T(8,128)(2,1)} %get-tuple-element.86.in_ref, bf16[4,128,1536]{2,1,0:T(8,128)(2,1)} %copy-done.11, bf16[4,128,1536]{2,1,0:T(8,128)(2,1)} %collective-permute-done.13.other_ref, bf16[4,576,256]{2,1,0:T(8,128)(2,1)} %get-tuple-element.85.d_ref, ...), custom_call_target="tpu_custom_call" | custom-call | flops 2415919104 | bytes 6291456 | tf_op jit(solution)/shard_map/pallas_call | solution.py:1005
  257.7 4.9 %all-to-all-done.5.d_ref = bf16[4,576,256]{2,1,0:T(8,128)(2,1)} async-done(((bf16[4,576,256]{2,1,0:T(8,128)(2,1)}), bf16[4,576,256]{2,1,0:T(8,128)(2,1)}, u32[]{:S(2)}, u32[]{:S(2)}) %all-to-all-start.5) | async-done | bytes 1179680 | tf_op jit(solution)/shard_map/all_to_all | solution.py:542
  265.6 7.0 %shard_map.390 = f32[256,1536]{1,0:T(8,128)} custom-call(bf16[4,576,256]{2,1,0:T(8,128)(2,1)} %all-to-all-done.5.d_ref, bf16[1536,768]{1,0:T(8,128)(2,1)} %qw_ref.1, bf16[1536,768]{1,0:T(8,128)(2,1)} %kw_ref.1, bf16[1536,768]{1,0:T(8,128)(2,1)} %vw_ref.1), custom_call_target="tpu_custom_call" | custom-call | flops 1811939328 | bytes 7077888 | tf_op jit(solution)/shard_map/pallas_call | solution.py:971
  284.5 4.4 %all-to-all-start.8 = ((bf16[4,96,1536]{2,1,0:T(8,128)(2,1)}), bf16[4,96,1536]{2,1,0:T(8,128)(2,1)}, u32[]{:S(2)}, u32[]{:S(2)}) async-start(bf16[4,96,1536]{2,1,0:T(8,128)(2,1)} %bitcast.126), calls=%async_computation.9 | async-start | bytes 2359296 | tf_op jit(solution)/shard_map/all_to_all | solution.py:542
  304.9 4.9 %all-to-all-start.7 = ((bf16[4,64,1536]{2,1,0:T(8,128)(2,1)}), bf16[4,64,1536]{2,1,0:T(8,128)(2,1)S(1)}, u32[]{:S(2)}, u32[]{:S(2)}) async-start(bf16[4,64,1536]{2,1,0:T(8,128)(2,1)} %pad_maximum_fusion.3), calls=%async_computation.7 | async-start | bytes 1572864 | tf_op jit(solution)/shard_map/all_to_all | solution.py:542
  314.1 11.9 %collective-permute-done.31.refs_3_ = bf16[256,1024]{1,0:T(8,128)(2,1)S(1)} collective-permute-done((bf16[256,1024]{1,0:T(8,128)(2,1)}, bf16[256,1024]{1,0:T(8,128)(2,1)S(1)}, u32[]{:S(2)}, u32[]{:S(2)}) %collective-permute-start.31) | collective-permute-done | bytes 524320 | tf_op jit(solution)/shard_map/ppermute | solution.py:494
  326.0 8.3 %collective-permute-done.30.refs_2_ = bf16[256,1024]{1,0:T(8,128)(2,1)S(1)} collective-permute-done((bf16[256,1024]{1,0:T(8,128)(2,1)}, bf16[256,1024]{1,0:T(8,128)(2,1)S(1)}, u32[]{:S(2)}, u32[]{:S(2)}) %collective-permute-start.30) | collective-permute-done | bytes 524320 | tf_op jit(solution)/shard_map/ppermute | solution.py:494
  339.6 11.8 %all-to-all-done.7 = bf16[4,64,1536]{2,1,0:T(8,128)(2,1)S(1)} async-done(((bf16[4,64,1536]{2,1,0:T(8,128)(2,1)}), bf16[4,64,1536]{2,1,0:T(8,128)(2,1)S(1)}, u32[]{:S(2)}, u32[]{:S(2)}) %all-to-all-start.7) | async-done | bytes 786464 | tf_op jit(solution)/shard_map/all_to_all | solution.py:542
  359.3 4.6 %all-to-all-done.11 = bf16[4,384,256]{2,1,0:T(8,128)(2,1)S(1)} async-done(((bf16[4,384,256]{2,1,0:T(8,128)(2,1)}), bf16[4,384,256]{2,1,0:T(8,128)(2,1)S(1)}, u32[]{:S(2)}, u32[]{:S(2)}) %all-to-all-start.11) | async-done | bytes 786464 | tf_op jit(solution)/shard_map/all_to_all | solution.py:542
  380.4 4.8 %fusion.16 = f32[64,4096]{1,0:T(8,128)S(1)} fusion(bf16[4096,768]{1,0:T(8,128)(2,1)} %param.41, bf16[768,128]{1,0:T(8,128)(2,1)S(1)} %bitcast.120), kind=kOutput, calls=%fused_computation.68 | convolution fusion | flops 402653184 | bytes 7536640 | tf_op jit(solution)/shard_map/dot_general | solution.py:546
  385.2 5.0 %convolution_add_fusion = f32[64,4096]{1,0:T(8,128)S(1)} fusion(f32[64,4096]{1,0:T(8,128)S(1)} %fusion.16, bf16[4096,768]{1,0:T(8,128)(2,1)} %param.42, bf16[768,128]{1,0:T(8,128)(2,1)S(1)} %bitcast.121), kind=kOutput, calls=%fused_computation | convolution fusion | flops 402915328 | bytes 8585216 | tf_op jit(solution)/shard_map/dot_general | solution.py:546
  (376 shorter events, 196.3 us)
Async XLA Ops:
  10.4 26.5 %all-to-all-start = ((bf16[4,64,1536]{2,1,0:T(8,128)(2,1)}), bf16[4,64,1536]{2,1,0:T(8,128)(2,1)}, u32[]{:S(2)}, u32[]{:S(2)}) async-start(bf16[4,64,1536]{2,1,0:T(8,128)(2,1)} %pad_maximum_fusion.1), calls=%async_computation | async-start | bytes 1572864 | tf_op jit(solution)/shard_map/all_to_all | solution.py:542
  48.1 16.4 %collective-permute-start.2 = (bf16[256,1536]{1,0:T(8,128)(2,1)}, bf16[256,1536]{1,0:T(8,128)(2,1)}, u32[]{:S(2)}, u32[]{:S(2)}) collective-permute-start(bf16[256,1536]{1,0:T(8,128)(2,1)} %get-tuple-element.169), channel_id=1, source_target_pairs={{0,4},{1,3},{2,6},{3,1},{4,0},{5,7},{6,2},{7,5},{8,12},{9,11},{10,... | collective-permute-start | bytes 2359304 | tf_op jit(solution)/shard_map/ppermute | solution.py:494
  55.7 56.6 %all-gather.2.cloned.1.call-start = ((), (), s32[]{:S(2)}) async-start(), calls=%async_computation.14 | async-start | bytes 3538944 | tf_op jit(solution)/shard_map/all_gather | solution.py:1236
  115.6 19.2 %all-to-all-start.3 = ((bf16[4,64,1024]{2,1,0:T(8,128)(2,1)}), bf16[4,64,1024]{2,1,0:T(8,128)(2,1)}, u32[]{:S(2)}, u32[]{:S(2)}) async-start(bf16[4,64,1024]{2,1,0:T(8,128)(2,1)} %shard_map.385), calls=%async_computation.3 | async-start | bytes 1048576 | tf_op jit(solution)/shard_map/all_to_all | solution.py:542
  120.2 164.3 %reduce-scatter.3.cloned.1.call-start = ((), (), s32[]{:S(2)}) async-start(), calls=%async_computation.15 | async-start | bytes 5898240 | tf_op jit(solution)/shard_map/reduce_scatter | solution.py:1309
  157.7 15.1 %collective-permute-start.9 = (bf16[512,1536]{1,0:T(8,128)(2,1)S(1)}, bf16[512,1536]{1,0:T(8,128)(2,1)S(1)}, u32[]{:S(2)}, u32[]{:S(2)}) collective-permute-start(bf16[512,1536]{1,0:T(8,128)(2,1)S(1)} %slice.429), channel_id=1, source_target_pairs={{0,1},{1,0},{2,3},{3,2},{4,5},{5,4},{6,7},{7,6},{8,9},{9,8},{10,11... | collective-permute-start | bytes 4718600 | tf_op jit(solution)/shard_map/ppermute | solution.py:494
  220.0 22.2 %all-to-all-start.6 = ((bf16[4,128,1536]{2,1,0:T(8,128)(2,1)}), bf16[4,128,1536]{2,1,0:T(8,128)(2,1)S(1)}, u32[]{:S(2)}, u32[]{:S(2)}) async-start(bf16[4,128,1536]{2,1,0:T(8,128)(2,1)} %broadcast_in_dim.38), calls=%async_computation.6 | async-start | bytes 3145728 | tf_op jit(solution)/shard_map/all_to_all | solution.py:542
  242.2 20.3 %all-to-all-start.5 = ((bf16[4,576,256]{2,1,0:T(8,128)(2,1)}), bf16[4,576,256]{2,1,0:T(8,128)(2,1)}, u32[]{:S(2)}, u32[]{:S(2)}) async-start(bf16[4,576,256]{2,1,0:T(8,128)(2,1)} %get-tuple-element.85.d_ref), calls=%async_computation.5 | async-start | bytes 2359296 | tf_op jit(solution)/shard_map/all_to_all | solution.py:542
  264.1 17.1 %collective-permute-start.14 = (bf16[256,1536]{1,0:T(8,128)(2,1)S(1)}, bf16[256,1536]{1,0:T(8,128)(2,1)}, u32[]{:S(2)}, u32[]{:S(2)}) collective-permute-start(bf16[256,1536]{1,0:T(8,128)(2,1)S(1)} %slice.780), channel_id=1, source_target_pairs={{0,4},{1,3},{2,6},{3,1},{4,0},{5,7},{6,2},{7,5},{8,12},{9,11},{10,... | collective-permute-start | bytes 2359304 | tf_op jit(solution)/shard_map/ppermute | solution.py:494
  274.5 19.1 %collective-permute-start.20 = (bf16[4,192,128]{2,1,0:T(8,128)(2,1)}, bf16[4,192,128]{2,1,0:T(8,128)(2,1)}, u32[]{:S(2)}, u32[]{:S(2)}) collective-permute-start(bf16[4,192,128]{2,1,0:T(8,128)(2,1)} %get-tuple-element.93.refs_4_), channel_id=1, source_target_pairs={{0,24},{1,25},{2,26},{3,27},{4,28},{5,29},{6,30},{7,31},{8,16},{9,... | collective-permute-start | bytes 589832 | tf_op jit(solution)/shard_map/ppermute | solution.py:494
  278.1 17.8 %collective-permute-start.19 = (bf16[4,192,128]{2,1,0:T(8,128)(2,1)}, bf16[4,192,128]{2,1,0:T(8,128)(2,1)}, u32[]{:S(2)}, u32[]{:S(2)}) collective-permute-start(bf16[4,192,128]{2,1,0:T(8,128)(2,1)} %get-tuple-element.93.refs_4_), channel_id=1, source_target_pairs={{0,16},{1,17},{2,18},{3,19},{4,20},{5,21},{6,22},{7,23},{8,24},{9,... | collective-permute-start | bytes 589832 | tf_op jit(solution)/shard_map/ppermute | solution.py:494
  278.1 17.8 %collective-permute-start.18 = (bf16[4,192,128]{2,1,0:T(8,128)(2,1)}, bf16[4,192,128]{2,1,0:T(8,128)(2,1)}, u32[]{:S(2)}, u32[]{:S(2)}) collective-permute-start(bf16[4,192,128]{2,1,0:T(8,128)(2,1)} %get-tuple-element.93.refs_4_), channel_id=1, source_target_pairs={{0,8},{1,9},{2,10},{3,11},{4,12},{5,13},{6,14},{7,15},{8,0},{9,1},... | collective-permute-start | bytes 589832 | tf_op jit(solution)/shard_map/ppermute | solution.py:494
  284.5 20.4 %all-to-all-start.8 = ((bf16[4,96,1536]{2,1,0:T(8,128)(2,1)}), bf16[4,96,1536]{2,1,0:T(8,128)(2,1)}, u32[]{:S(2)}, u32[]{:S(2)}) async-start(bf16[4,96,1536]{2,1,0:T(8,128)(2,1)} %bitcast.126), calls=%async_computation.9 | async-start | bytes 2359296 | tf_op jit(solution)/shard_map/all_to_all | solution.py:542
  289.0 82.9 %reduce-scatter.5.cloned.1.call-start = ((), (), s32[]{:S(2)}) async-start(), calls=%async_computation.16 | async-start | bytes 2949120 | tf_op jit(solution)/shard_map/reduce_scatter | solution.py:1311
  297.5 15.5 %collective-permute-start.25 = (f32[6912]{0:T(1024)S(1)}, f32[6912]{0:T(1024)S(1)}, u32[]{:S(2)}, u32[]{:S(2)}) collective-permute-start(f32[6912]{0:T(1024)S(1)} %concatenate.220), channel_id=1, source_target_pairs={{0,6},{1,7},{2,4},{3,5},{4,2},{5,3},{6,0},{7,1},{8,14},{9,15},{10,... | collective-permute-start | bytes 82952 | tf_op jit(solution)/shard_map/ppermute | solution.py:494
  304.9 46.5 %all-to-all-start.7 = ((bf16[4,64,1536]{2,1,0:T(8,128)(2,1)}), bf16[4,64,1536]{2,1,0:T(8,128)(2,1)S(1)}, u32[]{:S(2)}, u32[]{:S(2)}) async-start(bf16[4,64,1536]{2,1,0:T(8,128)(2,1)} %pad_maximum_fusion.3), calls=%async_computation.7 | async-start | bytes 1572864 | tf_op jit(solution)/shard_map/all_to_all | solution.py:542
  310.0 16.0 %collective-permute-start.31 = (bf16[256,1024]{1,0:T(8,128)(2,1)}, bf16[256,1024]{1,0:T(8,128)(2,1)S(1)}, u32[]{:S(2)}, u32[]{:S(2)}) collective-permute-start(bf16[256,1024]{1,0:T(8,128)(2,1)} %bitcast.21.refs_0_), channel_id=1, source_target_pairs={{0,6},{1,7},{2,4},{3,5},{4,2},{5,3},{6,0},{7,1},{8,14},{9,15},{10,... | collective-permute-start | bytes 1572872 | tf_op jit(solution)/shard_map/ppermute | solution.py:494
  311.4 22.8 %collective-permute-start.30 = (bf16[256,1024]{1,0:T(8,128)(2,1)}, bf16[256,1024]{1,0:T(8,128)(2,1)S(1)}, u32[]{:S(2)}, u32[]{:S(2)}) collective-permute-start(bf16[256,1024]{1,0:T(8,128)(2,1)} %bitcast.21.refs_0_), channel_id=1, source_target_pairs={{0,4},{1,5},{2,6},{3,7},{4,0},{5,1},{6,2},{7,3},{8,12},{9,13},{10,... | collective-permute-start | bytes 1572872 | tf_op jit(solution)/shard_map/ppermute | solution.py:494
  313.0 21.3 %collective-permute-start.29 = (bf16[256,1024]{1,0:T(8,128)(2,1)}, bf16[256,1024]{1,0:T(8,128)(2,1)S(1)}, u32[]{:S(2)}, u32[]{:S(2)}) collective-permute-start(bf16[256,1024]{1,0:T(8,128)(2,1)} %bitcast.21.refs_0_), channel_id=1, source_target_pairs={{0,2},{1,3},{2,0},{3,1},{4,6},{5,7},{6,4},{7,5},{8,10},{9,11},{10,... | collective-permute-start | bytes 1572872 | tf_op jit(solution)/shard_map/ppermute | solution.py:494
  354.9 14.9 %collective-permute-start.17 = (bf16[4,64,1536]{2,1,0:T(8,128)(2,1)S(1)}, bf16[4,64,1536]{2,1,0:T(8,128)(2,1)S(1)}, u32[]{:S(2)}, u32[]{:S(2)}) collective-permute-start(bf16[4,64,1536]{2,1,0:T(8,128)(2,1)S(1)} %all-to-all-done.7), channel_id=1, source_target_pairs={{0,1},{1,0},{2,3},{3,2},{4,5},{5,4},{6,7},{7,6},{8,9},{9,8},{10,11... | collective-permute-start | bytes 2359304 | tf_op jit(solution)/shard_map/ppermute | solution.py:494
  371.8 19.5 %collective-permute-start.28 = (f32[9216]{0:T(1024)S(1)}, f32[9216]{0:T(1024)S(1)}, u32[]{:S(2)}, u32[]{:S(2)}) collective-permute-start(f32[9216]{0:T(1024)S(1)} %pad_maximum_fusion.8), channel_id=1, source_target_pairs={{0,8},{1,9},{2,10},{3,11},{4,12},{5,13},{6,14},{7,15},{8,0},{9,1},... | collective-permute-start | bytes 110600 | tf_op jit(solution)/shard_map/ppermute | solution.py:494
  371.8 19.5 %collective-permute-start.27 = (f32[9216]{0:T(1024)S(1)}, f32[9216]{0:T(1024)S(1)}, u32[]{:S(2)}, u32[]{:S(2)}) collective-permute-start(f32[9216]{0:T(1024)S(1)} %pad_maximum_fusion.8), channel_id=1, source_target_pairs={{0,16},{1,17},{2,18},{3,19},{4,20},{5,21},{6,22},{7,23},{8,24},{9,... | collective-permute-start | bytes 110600 | tf_op jit(solution)/shard_map/ppermute | solution.py:494
  373.8 17.5 %collective-permute-start.26 = (f32[9216]{0:T(1024)S(1)}, f32[9216]{0:T(1024)S(1)}, u32[]{:S(2)}, u32[]{:S(2)}) collective-permute-start(f32[9216]{0:T(1024)S(1)} %pad_maximum_fusion.8), channel_id=1, source_target_pairs={{0,24},{1,25},{2,26},{3,27},{4,28},{5,29},{6,30},{7,31},{8,16},{9,... | collective-permute-start | bytes 110600 | tf_op jit(solution)/shard_map/ppermute | solution.py:494
  376.2 20.6 %all-to-all-start.10 = ((bf16[4,96,768]{2,1,0:T(8,128)(2,1)}), bf16[4,96,768]{2,1,0:T(8,128)(2,1)S(1)}, u32[]{:S(2)}, u32[]{:S(2)}) async-start(bf16[4,96,768]{2,1,0:T(8,128)(2,1)} %bitcast.131), calls=%async_computation.12 | async-start | bytes 1179648 | tf_op jit(solution)/shard_map/all_to_all | solution.py:542
  (94 other events, 747.6 us)
Sparse Core Ops, SparseCore 0:
  68.1 35.2 all-gather.1
  180.4 85.1 reduce-scatter.2
  296.1 59.5 reduce-scatter.4
where the time goes:
time: 409 us; the launch traced here: 407 us
  waiting for transfers between devices  98 us (24%)
  Pallas kernels  83 us (20%)
  starting transfers between devices  74.3 us (18%)
  local copies, waits for them, and re-layouts  52.9 us (13%)
  other arithmetic  48.1 us (12%)
  matrix products  22.9 us (6%)
  between operations  17 us (4%)
  blocking collectives  10.8 us (3%)
    ppermute x32, waiting for transfers between devices, move(): return lax.ppermute(value, MESH_AXES, pairs)  49.5 us
    all_to_all x11, waiting for transfers between devices, across(): return lax.all_to_all(value, axes, split, concat, tiled=True)  48.4 us
    all_to_all x11, starting transfers between devices, across(): return lax.all_to_all(value, axes, split, concat, tiled=True)  46.5 us
    ppermute x32, starting transfers between devices, move(): return lax.ppermute(value, MESH_AXES, pairs)  27.7 us
    dot_general x6, matrix products, contract(): lax.dot_general(left, right, (((left_dim,), (right_dim,)), ((), ())), pre...  17.4 us
    unnamed x147, local copies, waits for them, and re-layouts  15.9 us
    pallas_call x1, Pallas kernels, strip_shards(): attention_call(heads, lanes, texts, True)(*common, *saved, d_comb)  15.7 us
    pallas_call x1, Pallas kernels, ffn(): pl.pallas_call(ffn_kernel, grid_spec=pltpu.PrefetchScalarGridSpec(num_sca...  14.5 us
  transfers between devices with their start and end apart: 46, of which 22 were waited for; matrix products, arithmetic and copies ran while one was open for 24% of the time, Pallas kernels for 17%

commit v1 on v0

--- a/solution.py
+++ b/solution.py
@@ -1038,20 +1038,17 @@
     )(states)
 
 
-def text_grad_kernel(where_ref, *refs):
-    states, d_text, out_ref = refs[:PLANE], refs[PLANE : 2 * PLANE], refs[2 * PLANE]
-    own = where_ref[1]
+def text_grad_kernel(where_ref, states, *refs):
+    d_text, out_ref = refs[:STRIPS], refs[STRIPS]
+    own = where_ref[0]
     part = d_text[0].shape[2] // 2
     total = 0.0
-    for mask in range(PLANE):
-        place = where_ref[0] ^ mask
+    for place in range(PLANE):
         blocks = [
             jnp.concatenate([piece[place, :, :part], piece[place, :, part:]]) for piece in d_text
         ]
-        rows = [
-            states[mask][pl.ds(pl.multiple_of((own ^ strip) * part, part), part), :]
-            for strip in range(STRIPS)
-        ]
+        starts = [(place * STRIPS + (own ^ strip)) * part for strip in range(STRIPS)]
+        rows = [states[pl.ds(pl.multiple_of(start, part), part), :] for start in starts]
         total += jnp.dot(
             jnp.concatenate(blocks, axis=-1),
             jnp.concatenate(rows),
@@ -1062,18 +1059,18 @@
         out_ref[place] = total[:, place * size : (place + 1) * size].astype(jnp.bfloat16)
 
 
-def text_weight_grad(where_here, states, strips):
-    rows, cols = states[0].shape
+def text_weight_grad(strip, states, strips):
+    rows, cols = states.shape
     wide = 2 * strips[0].shape[1]
     whole = pl.BlockSpec(memory_space=pltpu.VMEM)
     return pl.pallas_call(
         text_grad_kernel,
-        in_specs=[pl.BlockSpec(memory_space=pltpu.SMEM)] + [whole] * 8,
+        in_specs=[pl.BlockSpec(memory_space=pltpu.SMEM)] + [whole] * 5,
         out_specs=whole,
         out_shape=jax.ShapeDtypeStruct((PLANE, wide, cols // PLANE), jnp.bfloat16),
         compiler_params=params(),
-        cost_estimate=cost(8 * rows * cols * wide, 8 * rows * cols),
-    )(where_here, *states, *strips)
+        cost_estimate=cost(2 * rows * cols * wide, 2 * rows * cols),
+    )(strip, states, *strips)
 
 
 def split_three(value):
@@ -1261,6 +1258,7 @@
     states = by_strips(after(text_states, own_ffn_in))
     states = across(states, "z", 0, 0).reshape(texts, states_wide)
     ffn_in = plane_gather(own_ffn_in, (states,))
+    states = lax.all_gather(states, PLANE_AXES, axis=0, tiled=True)
     inner, d_ffn_in = ffn(spot, ffn_in, d_ffn, gate_weight, up_weight, down_weight)
     ffn_grads, ffn_branch = ffn_grad(spot, ffn_in, d_ffn, inner, down_weight)
     branch_half = core_half(ffn_branch)
@@ -1306,12 +1304,11 @@
             [blocks[i, :, start : start + size] for i in range(PLANE)], axis=1
         ).astype(f32)
 
-    ffn_own = lax.psum_scatter(ffn_grads, "z", scatter_dimension=0, tiled=True)
+    ffn_own = lax.psum_scatter(after(ffn_grads, states), "z", scatter_dimension=0, tiled=True)
     d_text_all = gather_by(d_text, FLIP_STRIP)
     attn_grads = lax.psum_scatter(after(attn_grads, ffn_own, d_text_all), "z", scatter_dimension=0, tiled=True)
     ffn_blocks = spread(ffn_own)
     attn_blocks = spread(attn_grads)
-    block_out, tokens_grad = from_items(ffn_blocks, block_out, tokens_grad.astype(b16))
     gate_grad = sheet(ffn_blocks, 0, hidden_wide)
     up_grad = sheet(ffn_blocks, hidden_wide, hidden_wide)
     down_grad = sheet(ffn_blocks, 2 * hidden_wide, hidden_wide).T
@@ -1321,16 +1318,16 @@
     value_grad = sheet(attn_blocks, 2 * wide, wide)
 
     back = across(after(d_text, chip_d_qkv), PLANE_AXES, 0, 0)
-    back = after(back, attn_grads).reshape(-1, 2 * text_own)
+    back = back.reshape(-1, 2 * text_own)
     back = [back[:, :text_own], back[:, text_own:]]
-    text_grad = core_scatter(
-        contract(back[0], text_key_weight, 0, 1) + contract(back[1], text_value_weight, 0, 1), 1
-    )
-    states = gather_by(after(states, d_qkv), FLIP_PLACE)
-    where_here = jnp.stack([place, strip]).astype(jnp.int32)
-    states[0] = after(states[0], ffn_blocks)
+    text_part = contract(back[0], text_key_weight, 0, 1)
+    text_part = text_part + contract(back[1], text_value_weight, 0, 1)
+    text_grad = core_scatter(text_part, 1)
+    where_here = jnp.stack([strip]).astype(jnp.int32)
+    states = after(states, ffn_blocks)
     text_sum = text_weight_grad(where_here, states, d_text_all)
     text_blocks = across(text_sum, PLANE_AXES, 0, 0)
+    block_out, tokens_grad = from_items((ffn_blocks, text_part, text_blocks, attn_grads), block_out, tokens_grad.astype(b16))
     text_key_grad = text_blocks[:, :wide].reshape(PLANE * wide, -1).T.astype(f32)
     text_value_grad = text_blocks[:, wide:].reshape(PLANE * wide, -1).T.astype(f32)
 

time: 409 us -> 392 us (0.958)
  waiting for transfers between devices: 98 us -> 89.6 us
  local copies, waits for them, and re-layouts: 52.9 us -> 48 us
    ppermute x32 -> x29, waiting for transfers between devices: 49.5 us -> 29.3 us  [move(): return lax.ppermute(value, MESH_AXES, pairs)]
    all_to_all x11, waiting for transfers between devices: 48.4 us -> 60.2 us  [across(): return lax.all_to_all(value, axes, split, concat, tiled=True)]
    unnamed x147 -> x153, local copies, waits for them, and re-layouts: 15.9 us -> 10.4 us
    ppermute x32 -> x29, starting transfers between devices: 27.7 us -> 26.3 us  [move(): return lax.ppermute(value, MESH_AXES, pairs)]
  transfers between devices with their start and end apart: 46 -> 44, of which waited for: 22 -> 19; matrix products, arithmetic and copies ran while one was open for 24% -> 25% of each run, Pallas kernels for 17% -> 21%
where the time goes in v1:
time: 392 us; the launch traced here: 390 us
  waiting for transfers between devices  89.6 us (23%)
  Pallas kernels  83.2 us (21%)
  starting transfers between devices  71.7 us (18%)
  local copies, waits for them, and re-layouts  48 us (12%)
  other arithmetic  47 us (12%)
  matrix products  23 us (6%)
  between operations  17 us (4%)
  blocking collectives  10.8 us (3%)
    all_to_all x11, waiting for transfers between devices, across(): return lax.all_to_all(value, axes, split, concat, tiled=True)  60.2 us
    all_to_all x11, starting transfers between devices, across(): return lax.all_to_all(value, axes, split, concat, tiled=True)  45.3 us
    ppermute x29, waiting for transfers between devices, move(): return lax.ppermute(value, MESH_AXES, pairs)  29.3 us
    ppermute x29, starting transfers between devices, move(): return lax.ppermute(value, MESH_AXES, pairs)  26.3 us
    dot_general x6, matrix products, contract(): lax.dot_general(left, right, (((left_dim,), (right_dim,)), ((), ())), pre...  17.5 us
    pallas_call x1, Pallas kernels, strip_shards(): attention_call(heads, lanes, texts, True)(*common, *saved, d_comb)  15.8 us
    pallas_call x1, Pallas kernels, ffn(): pl.pallas_call(ffn_kernel, grid_spec=pltpu.PrefetchScalarGridSpec(num_sca...  14.6 us
    pallas_call x1, Pallas kernels, ffn_grad(): pl.pallas_call(ffn_grad_kernel, grid_spec=pltpu.PrefetchScalarGridSpec(nu...  11.9 us
  transfers between devices with their start and end apart: 44, of which 19 were waited for; matrix products, arithmetic and copies ran while one was open for 25% of the time, Pallas kernels for 21%

profile of v1, /device:TPU:0, one launch (start us, length us, event | category | flops | bytes accessed | tf_op | source)
XLA Modules:
  0.0 390.2 jit_solution(16832478015890181868)
XLA Ops:
  10.4 6.3 %all-to-all-start = ((bf16[4,64,1536]{2,1,0:T(8,128)(2,1)}), bf16[4,64,1536]{2,1,0:T(8,128)(2,1)}, u32[]{:S(2)}, u32[]{:S(2)}) async-start(bf16[4,64,1536]{2,1,0:T(8,128)(2,1)} %pad_maximum_fusion.1), calls=%async_computation | async-start | bytes 1572864 | tf_op jit(solution)/shard_map/all_to_all | solution.py:542
  17.6 4.1 %fusion.97 = f32[768,64]{0,1:T(8,128)S(1)} fusion(bf16[64,4096]{1,0:T(8,128)(2,1)S(1)} %copy-done.12, bf16[4096,768]{1,0:T(8,128)(2,1)} %param.41), kind=kOutput, calls=%fused_computation.321 | convolution fusion | flops 402653184 | bytes 7012352 | tf_op jit(solution)/shard_map/dot_general | solution.py:546
  60.6 3.9 all-to-all-done.1.text_ref
  72.2 8.4 %shard_map.383 = (bf16[1024,1536]{1,0:T(8,128)(2,1)}, f32[576,1024]{1,0:T(8,128)}) custom-call(s32[10]{0:T(128)} %stack.65.spot_ref, bf16[512,1536]{1,0:T(8,128)(2,1)} %constant_dynamic-update-slice_fusion.2.own_ref, bf16[512,1536]{1,0:T(8,128)(2,1)} %collective-permute-done.3.other_ref, f32[1,1536]{1,0:T(1,128)} %broadcast_in_dim.37.lift_ref, ...), custom_call_target="tpu_custom_call" | custom-call | flops 1811939328 | bytes 12582912 | tf_op jit(solution)/shard_map/pallas_call | solution.py:818
  80.6 11.6 %shard_map.384 = (bf16[4,192,256]{2,1,0:T(8,128)(2,1)}, f32[192,1024]{1,0:T(8,128)}, f32[192,1024]{1,0:T(8,128)}, bf16[192,1024]{1,0:T(8,128)(2,1)}, bf16[192,10...) custom-call(s32[10]{0:T(128)} %stack.65.spot_ref, f32[576,1024]{1,0:T(8,128)} %get-tuple-element.66.q_ref.k_ref.v_ref, ...), custom_call_target="tpu_custom_call" | custom-call | flops 4026531840 | bytes 1572864 | tf_op jit(solution)/shard_map/pallas_call | solution.py:1247
  96.0 7.4 %all-to-all-done.2 = bf16[4,192,256]{2,1,0:T(8,128)(2,1)S(1)} async-done(((bf16[4,192,256]{2,1,0:T(8,128)(2,1)}), bf16[4,192,256]{2,1,0:T(8,128)(2,1)S(1)}, u32[]{:S(2)}, u32[]{:S(2)}) %all-to-all-start.2) | async-done | bytes 393248 | tf_op jit(solution)/shard_map/all_to_all | solution.py:542
  114.8 4.6 %all-to-all-start.3 = ((bf16[4,64,1024]{2,1,0:T(8,128)(2,1)}), bf16[4,64,1024]{2,1,0:T(8,128)(2,1)}, u32[]{:S(2)}, u32[]{:S(2)}) async-start(bf16[4,64,1024]{2,1,0:T(8,128)(2,1)} %shard_map.385), calls=%async_computation.3 | async-start | bytes 1048576 | tf_op jit(solution)/shard_map/all_to_all | solution.py:542
  125.7 8.3 %all-to-all-done.3 = bf16[4,64,1024]{2,1,0:T(8,128)(2,1)} async-done(((bf16[4,64,1024]{2,1,0:T(8,128)(2,1)}), bf16[4,64,1024]{2,1,0:T(8,128)(2,1)}, u32[]{:S(2)}, u32[]{:S(2)}) %all-to-all-start.3) | async-done | bytes 524320 | tf_op jit(solution)/shard_map/all_to_all | solution.py:542
  139.9 14.6 %shard_map.386 = (bf16[1024,1536]{1,0:T(8,128)(2,1)}, bf16[1024,1536]{1,0:T(8,128)(2,1)}) custom-call(s32[10]{0:T(128)} %stack.65.spot_ref, bf16[512,1536]{1,0:T(8,128)(2,1)} %constant_dynamic-update-slice_fusion.5.a_ref, bf16[512,1536]{1,0:T(8,128)(2,1)} %collective-permute-done.7.b_ref, ...), custom_call_target="tpu_custom_call" | custom-call | flops 8053063680 | bytes 12582912 | tf_op jit(solution)/shard_map/pallas_call | solution.py:871
  157.3 11.9 %shard_map.387 = (bf16[1536,1536]{1,0:T(8,128)(2,1)}, bf16[1024,1536]{1,0:T(8,128)(2,1)}) custom-call(s32[10]{0:T(128)} %stack.65.spot_ref, bf16[512,1536]{1,0:T(8,128)(2,1)} %constant_dynamic-update-slice_fusion.5.a_ref, bf16[512,1536]{1,0:T(8,128)(2,1)} %collective-permute-done.7.b_ref, ...), custom_call_target="tpu_custom_call" | custom-call | flops 6442450944 | bytes 12582912 | tf_op jit(solution)/shard_map/pallas_call | solution.py:920
  179.9 7.0 %collective-permute-done.10 = bf16[256,1536]{1,0:T(8,128)(2,1)S(1)} collective-permute-done((bf16[256,1536]{1,0:T(8,128)(2,1)S(1)}, bf16[256,1536]{1,0:T(8,128)(2,1)S(1)}, u32[]{:S(2)}, u32[]{:S(2)}) %collective-permute-start.10) | collective-permute-done | bytes 786464 | tf_op jit(solution)/shard_map/ppermute | solution.py:494
  188.7 6.3 %collective-permute-done.11 = bf16[128,1536]{1,0:T(8,128)(2,1)S(1)} collective-permute-done((bf16[128,1536]{1,0:T(8,128)(2,1)S(1)}, bf16[128,1536]{1,0:T(8,128)(2,1)S(1)}, u32[]{:S(2)}, u32[]{:S(2)}) %collective-permute-start.11) | collective-permute-done | bytes 393248 | tf_op jit(solution)/shard_map/ppermute | solution.py:494
  202.5 10.8 %all_to_all.60.dcomb_ref = bf16[4,192,256]{2,1,0:T(8,128)(2,1)} all-to-all(bf16[4,192,256]{2,1,0:T(8,128)(2,1)S(1)} %bitcast.123), channel_id=1, replica_groups=mesh['z'=4,'y'=2,'x'=2,'c'=2] {'y','x'}, dimensions={0} | all-to-all | bytes 786432 | tf_op jit(solution)/shard_map/all_to_all | solution.py:542
  218.4 15.8 %shard_map.388 = (bf16[4,576,256]{2,1,0:T(8,128)(2,1)}, bf16[4,192,128]{2,1,0:T(8,128)(2,1)}, f32[192,512]{1,0:T(8,128)}) custom-call(s32[10]{0:T(128)} %stack.65.spot_ref, f32[576,1024]{1,0:T(8,128)} %get-tuple-element.66.q_ref.k_ref.v_ref, f32[576,1024]{1,0:T(8,128)} %get-tuple-element.66.q_ref.k_ref.v_ref, ...), custom_call_target="tpu_custom_call" | custom-call | flops 10066329600 | bytes 1572864 | tf_op jit(solution)/shard_map/pallas_call | solution.py:1278
  238.5 4.3 %all-to-all-start.5 = ((bf16[4,576,256]{2,1,0:T(8,128)(2,1)}), bf16[4,576,256]{2,1,0:T(8,128)(2,1)}, u32[]{:S(2)}, u32[]{:S(2)}) async-start(bf16[4,576,256]{2,1,0:T(8,128)(2,1)} %get-tuple-element.84.d_ref), calls=%async_computation.5 | async-start | bytes 2359296 | tf_op jit(solution)/shard_map/all_to_all | solution.py:542
  249.8 8.3 %shard_map.389 = bf16[1536,768]{1,0:T(8,128)(2,1)} custom-call(s32[10]{0:T(128)} %stack.65.spot_ref, bf16[1024,1536]{1,0:T(8,128)(2,1)} %get-tuple-element.85.in_ref, bf16[4,128,1536]{2,1,0:T(8,128)(2,1)} %copy-done.8, bf16[4,128,1536]{2,1,0:T(8,128)(2,1)} %collective-permute-done.13.other_ref, bf16[4,576,256]{2,1,0:T(8,128)(2,1)} %get-tuple-element.84.d_ref, ...), custom_call_target="tpu_custom_call" | custom-call | flops 2415919104 | bytes 6291456 | tf_op jit(solution)/shard_map/pallas_call | solution.py:1005
  266.6 7.0 %shard_map.390 = f32[256,1536]{1,0:T(8,128)} custom-call(bf16[4,576,256]{2,1,0:T(8,128)(2,1)} %all-to-all-done.5.d_ref, bf16[1536,768]{1,0:T(8,128)(2,1)} %qw_ref.1, bf16[1536,768]{1,0:T(8,128)(2,1)} %kw_ref.1, bf16[1536,768]{1,0:T(8,128)(2,1)} %vw_ref.1), custom_call_target="tpu_custom_call" | custom-call | flops 1811939328 | bytes 7077888 | tf_op jit(solution)/shard_map/pallas_call | solution.py:971
  275.5 4.8 %fusion.16 = f32[64,4096]{1,0:T(8,128)S(1)} fusion(bf16[4096,768]{1,0:T(8,128)(2,1)} %param.41, bf16[768,128]{1,0:T(8,128)(2,1)S(1)} %bitcast.120), kind=kOutput, calls=%fused_computation.68 | convolution fusion | flops 402653184 | bytes 7536640 | tf_op jit(solution)/shard_map/dot_general | solution.py:546
  280.3 5.1 %convolution_add_fusion = f32[64,4096]{1,0:T(8,128)S(1)} fusion(f32[64,4096]{1,0:T(8,128)S(1)} %fusion.16, bf16[4096,768]{1,0:T(8,128)(2,1)} %param.42, bf16[768,128]{1,0:T(8,128)(2,1)S(1)} %bitcast.121), kind=kOutput, calls=%fused_computation | convolution fusion | flops 402915328 | bytes 8585216 | tf_op jit(solution)/shard_map/dot_general | solution.py:546
  293.4 5.2 %collective-permute-done.15 = bf16[128,1536]{1,0:T(8,128)(2,1)S(1)} collective-permute-done((bf16[128,1536]{1,0:T(8,128)(2,1)S(1)}, bf16[128,1536]{1,0:T(8,128)(2,1)S(1)}, u32[]{:S(2)}, u32[]{:S(2)}) %collective-permute-start.15) | collective-permute-done | bytes 393248 | tf_op jit(solution)/shard_map/ppermute | solution.py:494
  309.7 13.3 %all-to-all-done.8 = bf16[4,96,1536]{2,1,0:T(8,128)(2,1)S(1)} async-done(((bf16[4,96,1536]{2,1,0:T(8,128)(2,1)}), bf16[4,96,1536]{2,1,0:T(8,128)(2,1)S(1)}, u32[]{:S(2)}, u32[]{:S(2)}) %all-to-all-start.8) | async-done | bytes 1179680 | tf_op jit(solution)/shard_map/all_to_all | solution.py:542
  331.9 8.7 %all-to-all-done.10 = bf16[4,384,256]{2,1,0:T(8,128)(2,1)S(1)} async-done(((bf16[4,384,256]{2,1,0:T(8,128)(2,1)}), bf16[4,384,256]{2,1,0:T(8,128)(2,1)S(1)}, u32[]{:S(2)}, u32[]{:S(2)}) %all-to-all-start.10) | async-done | bytes 786464 | tf_op jit(solution)/shard_map/all_to_all | solution.py:542
  340.6 4.9 %all-to-all-start.7 = ((bf16[4,64,1536]{2,1,0:T(8,128)(2,1)}), bf16[4,64,1536]{2,1,0:T(8,128)(2,1)S(1)}, u32[]{:S(2)}, u32[]{:S(2)}) async-start(bf16[4,64,1536]{2,1,0:T(8,128)(2,1)} %pad_maximum_fusion.3), calls=%async_computation.7 | async-start | bytes 1572864 | tf_op jit(solution)/shard_map/all_to_all | solution.py:542
  355.1 12.1 %all-to-all-done.7 = bf16[4,64,1536]{2,1,0:T(8,128)(2,1)S(1)} async-done(((bf16[4,64,1536]{2,1,0:T(8,128)(2,1)}), bf16[4,64,1536]{2,1,0:T(8,128)(2,1)S(1)}, u32[]{:S(2)}, u32[]{:S(2)}) %all-to-all-start.7) | async-done | bytes 786464 | tf_op jit(solution)/shard_map/all_to_all | solution.py:542
  (378 shorter events, 178.6 us)
Async XLA Ops:
  10.4 26.5 %all-to-all-start = ((bf16[4,64,1536]{2,1,0:T(8,128)(2,1)}), bf16[4,64,1536]{2,1,0:T(8,128)(2,1)}, u32[]{:S(2)}, u32[]{:S(2)}) async-start(bf16[4,64,1536]{2,1,0:T(8,128)(2,1)} %pad_maximum_fusion.1), calls=%async_computation | async-start | bytes 1572864 | tf_op jit(solution)/shard_map/all_to_all | solution.py:542
  48.1 16.4 %collective-permute-start.2 = (bf16[256,1536]{1,0:T(8,128)(2,1)}, bf16[256,1536]{1,0:T(8,128)(2,1)}, u32[]{:S(2)}, u32[]{:S(2)}) collective-permute-start(bf16[256,1536]{1,0:T(8,128)(2,1)} %get-tuple-element.167), channel_id=1, source_target_pairs={{0,4},{1,3},{2,6},{3,1},{4,0},{5,7},{6,2},{7,5},{8,12},{9,11},{10,... | collective-permute-start | bytes 2359304 | tf_op jit(solution)/shard_map/ppermute | solution.py:494
  52.2 12.3 %all-to-all-start.1 = ((f32[4,192,128]{2,1,0:T(8,128)}), f32[4,192,128]{2,1,0:T(8,128)S(1)}, u32[]{:S(2)}, u32[]{:S(2)}) async-start(f32[4,192,128]{2,1,0:T(8,128)} %bitcast.4), calls=%async_computation.1 | async-start | bytes 786432 | tf_op jit(solution)/shard_map/all_to_all | solution.py:542
  55.7 55.8 %all-gather.3.cloned.1.call-start = ((), (), s32[]{:S(2)}) async-start(), calls=%async_computation.14 | async-start | bytes 3538944 | tf_op jit(solution)/shard_map/all_gather | solution.py:1233
  114.8 19.2 %all-to-all-start.3 = ((bf16[4,64,1024]{2,1,0:T(8,128)(2,1)}), bf16[4,64,1024]{2,1,0:T(8,128)(2,1)}, u32[]{:S(2)}, u32[]{:S(2)}) async-start(bf16[4,64,1024]{2,1,0:T(8,128)(2,1)} %shard_map.385), calls=%async_computation.3 | async-start | bytes 1048576 | tf_op jit(solution)/shard_map/all_to_all | solution.py:542
  119.4 52.8 %all-gather.5.cloned.1.call-start = ((), (), s32[]{:S(2)}) async-start(), calls=%async_computation.15 | async-start | bytes 2621440 | tf_op jit(solution)/shard_map/all_gather | solution.py:1261
  121.6 12.4 %collective-permute-start.6 = (bf16[256,1536]{1,0:T(8,128)(2,1)}, bf16[256,1536]{1,0:T(8,128)(2,1)}, u32[]{:S(2)}, u32[]{:S(2)}) collective-permute-start(bf16[256,1536]{1,0:T(8,128)(2,1)} %pad_maximum_fusion.2), channel_id=1, source_target_pairs={{0,4},{1,3},{2,6},{3,1},{4,0},{5,7},{6,2},{7,5},{8,12},{9,11},{10,... | collective-permute-start | bytes 2359304 | tf_op jit(solution)/shard_map/ppermute | solution.py:494
  136.1 152.5 %reduce-scatter.3.cloned.1.call-start = ((), (), s32[]{:S(2)}) async-start(), calls=%async_computation.16 | async-start | bytes 5898240 | tf_op jit(solution)/shard_map/reduce_scatter | solution.py:1307
  157.2 15.1 %collective-permute-start.9 = (bf16[512,1536]{1,0:T(8,128)(2,1)}, bf16[512,1536]{1,0:T(8,128)(2,1)}, u32[]{:S(2)}, u32[]{:S(2)}) collective-permute-start(bf16[512,1536]{1,0:T(8,128)(2,1)} %slice.429), channel_id=1, source_target_pairs={{0,1},{1,0},{2,3},{3,2},{4,5},{5,4},{6,7},{7,6},{8,9},{9,8},{10,11... | collective-permute-start | bytes 4718600 | tf_op jit(solution)/shard_map/ppermute | solution.py:494
  214.6 22.2 %all-to-all-start.6 = ((bf16[4,128,1536]{2,1,0:T(8,128)(2,1)}), bf16[4,128,1536]{2,1,0:T(8,128)(2,1)S(1)}, u32[]{:S(2)}, u32[]{:S(2)}) async-start(bf16[4,128,1536]{2,1,0:T(8,128)(2,1)} %broadcast_in_dim.38), calls=%async_computation.6 | async-start | bytes 3145728 | tf_op jit(solution)/shard_map/all_to_all | solution.py:542
  236.8 13.1 %collective-permute-start.13 = (bf16[4,128,1536]{2,1,0:T(8,128)(2,1)S(1)}, bf16[4,128,1536]{2,1,0:T(8,128)(2,1)}, u32[]{:S(2)}, u32[]{:S(2)}) collective-permute-start(bf16[4,128,1536]{2,1,0:T(8,128)(2,1)S(1)} %all-to-all-done.6.own_ref), channel_id=1, source_target_pairs={{0,1},{1,0},{2,3},{3,2},{4,5},{5,4},{6,7},{7,6},{8,9},{9,8},{10,11... | collective-permute-start | bytes 4718600 | tf_op jit(solution)/shard_map/ppermute | solution.py:494
  238.5 20.3 %all-to-all-start.5 = ((bf16[4,576,256]{2,1,0:T(8,128)(2,1)}), bf16[4,576,256]{2,1,0:T(8,128)(2,1)}, u32[]{:S(2)}, u32[]{:S(2)}) async-start(bf16[4,576,256]{2,1,0:T(8,128)(2,1)} %get-tuple-element.84.d_ref), calls=%async_computation.5 | async-start | bytes 2359296 | tf_op jit(solution)/shard_map/all_to_all | solution.py:542
  244.6 43.9 %collective-permute-start.19 = (bf16[4,192,128]{2,1,0:T(8,128)(2,1)}, bf16[4,192,128]{2,1,0:T(8,128)(2,1)}, u32[]{:S(2)}, u32[]{:S(2)}) collective-permute-start(bf16[4,192,128]{2,1,0:T(8,128)(2,1)} %get-tuple-element.92.refs_0_), channel_id=1, source_target_pairs={{0,24},{1,25},{2,26},{3,27},{4,28},{5,29},{6,30},{7,31},{8,16},{9,... | collective-permute-start | bytes 589832 | tf_op jit(solution)/shard_map/ppermute | solution.py:494
  248.2 40.3 %collective-permute-start.18 = (bf16[4,192,128]{2,1,0:T(8,128)(2,1)}, bf16[4,192,128]{2,1,0:T(8,128)(2,1)}, u32[]{:S(2)}, u32[]{:S(2)}) collective-permute-start(bf16[4,192,128]{2,1,0:T(8,128)(2,1)} %get-tuple-element.92.refs_0_), channel_id=1, source_target_pairs={{0,16},{1,17},{2,18},{3,19},{4,20},{5,21},{6,22},{7,23},{8,24},{9,... | collective-permute-start | bytes 589832 | tf_op jit(solution)/shard_map/ppermute | solution.py:494
  248.2 40.3 %collective-permute-start.17 = (bf16[4,192,128]{2,1,0:T(8,128)(2,1)}, bf16[4,192,128]{2,1,0:T(8,128)(2,1)}, u32[]{:S(2)}, u32[]{:S(2)}) collective-permute-start(bf16[4,192,128]{2,1,0:T(8,128)(2,1)} %get-tuple-element.92.refs_0_), channel_id=1, source_target_pairs={{0,8},{1,9},{2,10},{3,11},{4,12},{5,13},{6,14},{7,15},{8,0},{9,1},... | collective-permute-start | bytes 589832 | tf_op jit(solution)/shard_map/ppermute | solution.py:494
  258.8 16.7 %all-to-all-start.9 = ((bf16[4,192,128]{2,1,0:T(8,128)(2,1)}), bf16[4,192,128]{2,1,0:T(8,128)(2,1)S(1)}, u32[]{:S(2)}, u32[]{:S(2)}) async-start(bf16[4,192,128]{2,1,0:T(8,128)(2,1)} %get-tuple-element.92.refs_0_), calls=%async_computation.10 | async-start | bytes 393216 | tf_op jit(solution)/shard_map/all_to_all | solution.py:542
  262.2 85.4 %reduce-scatter.5.cloned.1.call-start = ((), (), s32[]{:S(2)}) async-start(), calls=%async_computation.17 | async-start | bytes 2949120 | tf_op jit(solution)/shard_map/reduce_scatter | solution.py:1309
  264.6 24.1 %collective-permute-start.14 = (bf16[256,1536]{1,0:T(8,128)(2,1)}, bf16[256,1536]{1,0:T(8,128)(2,1)}, u32[]{:S(2)}, u32[]{:S(2)}) collective-permute-start(bf16[256,1536]{1,0:T(8,128)(2,1)} %slice.780), channel_id=1, source_target_pairs={{0,4},{1,3},{2,6},{3,1},{4,0},{5,7},{6,2},{7,5},{8,12},{9,11},{10,... | collective-permute-start | bytes 2359304 | tf_op jit(solution)/shard_map/ppermute | solution.py:494
  304.4 18.6 %all-to-all-start.8 = ((bf16[4,96,1536]{2,1,0:T(8,128)(2,1)}), bf16[4,96,1536]{2,1,0:T(8,128)(2,1)S(1)}, u32[]{:S(2)}, u32[]{:S(2)}) async-start(bf16[4,96,1536]{2,1,0:T(8,128)(2,1)} %bitcast.126), calls=%async_computation.9 | async-start | bytes 2359296 | tf_op jit(solution)/shard_map/all_to_all | solution.py:542
  326.7 13.9 %all-to-all-start.10 = ((bf16[4,384,256]{2,1,0:T(8,128)(2,1)}), bf16[4,384,256]{2,1,0:T(8,128)(2,1)S(1)}, u32[]{:S(2)}, u32[]{:S(2)}) async-start(bf16[4,384,256]{2,1,0:T(8,128)(2,1)} %shard_map.391), calls=%async_computation.11 | async-start | bytes 1572864 | tf_op jit(solution)/shard_map/all_to_all | solution.py:542
  340.6 26.6 %all-to-all-start.7 = ((bf16[4,64,1536]{2,1,0:T(8,128)(2,1)}), bf16[4,64,1536]{2,1,0:T(8,128)(2,1)S(1)}, u32[]{:S(2)}, u32[]{:S(2)}) async-start(bf16[4,64,1536]{2,1,0:T(8,128)(2,1)} %pad_maximum_fusion.3), calls=%async_computation.7 | async-start | bytes 1572864 | tf_op jit(solution)/shard_map/all_to_all | solution.py:542
  348.2 22.5 %collective-permute-start.28 = (f32[9216]{0:T(1024)S(1)}, f32[9216]{0:T(1024)S(1)}, u32[]{:S(2)}, u32[]{:S(2)}) collective-permute-start(f32[9216]{0:T(1024)S(1)} %copy-done.26), channel_id=1, source_target_pairs={{0,8},{1,9},{2,10},{3,11},{4,12},{5,13},{6,14},{7,15},{8,0},{9,1},... | collective-permute-start | bytes 110600 | tf_op jit(solution)/shard_map/ppermute | solution.py:494
  350.2 20.5 %collective-permute-start.27 = (f32[9216]{0:T(1024)S(1)}, f32[9216]{0:T(1024)S(1)}, u32[]{:S(2)}, u32[]{:S(2)}) collective-permute-start(f32[9216]{0:T(1024)S(1)} %copy-done.26), channel_id=1, source_target_pairs={{0,16},{1,17},{2,18},{3,19},{4,20},{5,21},{6,22},{7,23},{8,24},{9,... | collective-permute-start | bytes 110600 | tf_op jit(solution)/shard_map/ppermute | solution.py:494
  352.6 18.2 %collective-permute-start.26 = (f32[9216]{0:T(1024)S(1)}, f32[9216]{0:T(1024)S(1)}, u32[]{:S(2)}, u32[]{:S(2)}) collective-permute-start(f32[9216]{0:T(1024)S(1)} %copy-done.26), channel_id=1, source_target_pairs={{0,24},{1,25},{2,26},{3,27},{4,28},{5,29},{6,30},{7,31},{8,16},{9,... | collective-permute-start | bytes 110600 | tf_op jit(solution)/shard_map/ppermute | solution.py:494
  (95 other events, 905.6 us)
Sparse Core Ops, SparseCore 0:
  68.1 32.8 all-gather.2
  136.3 35.7 all-gather.4
  174.3 93.3 reduce-scatter.2
  288.8 48.3 reduce-scatter.4
